TPU v7x, 32 devices: a whole 2x2x4 slice. The times are simulated.
32 devices in a mesh: gx: 4 (over z), gy: 8 (over y, x, core).
Axes of the slice: x: 2, y: 2, z: 4, core: 2. Of those that a mesh axis runs over, the one named last changes fastest.
Arguments:
- velocity: float32 [2, 2048, 4096], P(None, 'gx', 'gy'), may hold values from -6 to 6
- observed: float32 [2, 2048, 4096], P(None, 'gx', 'gy'), may hold values from -6 to 6
- thickness: float32 [2048, 4096], P('gx', 'gy'), may hold values from 0.5 to 2
- rate_factor: float32 [2048, 4096], P('gx', 'gy'), may hold values from 0.5 to 2
- friction: float32 [2048, 4096], P('gx', 'gy'), may hold values from 0.1 to 10
- cell_mask: int32 [2048, 4096], P('gx', 'gy'), may hold values from 0 to 2
- front_codes: int32 [2048, 4096], P('gx', 'gy'), may hold values from 0 to 15
- modes_x: bfloat16 [2048, 512], P('gx'), may hold values from -0.125 to 0.125
- modes_y: bfloat16 [4096, 512], P('gy'), may hold values from -0.09375 to 0.09375
Outputs:
- adjoint: float32 [2, 2048, 4096], P(None, 'gx', 'gy')
- coefficients: float32 [512, 512], P('gx', 'gy')
Inputs may be any that keep to these rules, and one draw needn't show every extreme that they name: `cell_mask`: 0 is ocean, 1 floating ice, 2 grounded ice. `front_codes`: bit 0, 1, 2, 3 marks a calving front on the cell's lower first-dimension, upper first-dimension, lower second-dimension, upper second-dimension face.
All inputs are finite; a program needn't handle non-finite values.
Results may differ from a plain program's by a relative error of at most 0.0029.
Values sent between devices are 32-bit elements; how exact they have to be, the bound alone decides.
A program may use at most 128 MiB of HBM per device.

v0:
```python
import functools

import jax
import jax.numpy as jnp
from jax import lax
from jax.experimental import pallas as pl
from jax.experimental.pallas import tpu as pltpu
from jax.sharding import PartitionSpec as P

SWEEPS = 3
ROWS = 64
LT = 128
VMEM_LIMIT = 48 * 1024 * 1024
MESH = pl.DeviceIdType.MESH
F32 = jnp.float32
BF16 = jnp.bfloat16


def kernel(
    ngx, ngy,
    vel_h, obs_h, thick_h, rate_h, fric_h, mask_h, codes_h, mx_h, my_h,
    adj, coef_ref,
    vel, obs, thick, rate, fric, mask, codes, mx, my,
    s_pad, q1, q2, p_f, g_f, e_f, grad, mxt, myt, t_hi, t_lo,
    edge_out, edge_in, halo, r_send, r_acc, r_in, half_in, z_out, z_in,
    vel_sem, load_sem, halo_send, halo_recv, col_send, col_recv,
    pair_send, pair_recv, half_send, half_recv, z_send, z_recv,
):
    h, w = thick.shape
    nt = w // LT
    ix, iy = lax.axis_index("gx"), lax.axis_index("gy")
    body = pl.ds(8, h)
    outer, inner = (0, nt - 1), tuple(range(1, nt - 1))

    vel_loads = [
        pltpu.make_async_copy(
            vel_h.at[:, :, pl.ds(t * LT, LT)], vel.at[:, t, body], vel_sem.at[t])
        for t in outer + inner
    ]
    loads = [
        pltpu.make_async_copy(thick_h, thick, load_sem.at[0]),
        pltpu.make_async_copy(rate_h, rate, load_sem.at[1]),
        pltpu.make_async_copy(mask_h, mask, load_sem.at[2]),
        pltpu.make_async_copy(fric_h, fric, load_sem.at[3]),
        pltpu.make_async_copy(codes_h, codes, load_sem.at[4]),
        pltpu.make_async_copy(obs_h, obs, load_sem.at[5]),
        pltpu.make_async_copy(mx_h, mx, load_sem.at[6]),
        pltpu.make_async_copy(my_h, my, load_sem.at[7]),
    ]
    for load in vel_loads + loads:
        load.start()

    barrier = pltpu.get_barrier_semaphore()
    for off in range(1, ngx):
        pl.semaphore_signal(barrier, inc=1, device_id=(lax.rem(ix + off, ngx), iy), device_id_type=MESH)
    for off in range(1, ngy):
        pl.semaphore_signal(barrier, inc=1, device_id=(ix, lax.rem(iy + off, ngy)), device_id_type=MESH)
    pl.semaphore_wait(barrier, ngx - 1 + ngy - 1)

    has_n, has_s, has_w, has_e = ix > 0, ix < ngx - 1, iy > 0, iy < ngy - 1

    fields = (vel, s_pad, q1, q2)

    for missing, rows in ((ix == 0, 0), (ix == ngx - 1, h + 8)):

        @pl.when(missing)
        def _(rows=rows):
            for ref in fields:
                ref[:, :, pl.ds(rows, 8)] = jnp.zeros((ref.shape[0], nt, 8, LT), F32)

    for missing, side in ((iy == 0, 0), (iy == ngy - 1, 1)):

        @pl.when(missing)
        def _(side=side):
            edge_in[:, side] = jnp.zeros((4, 8, h), F32)

    def copies_of(k):
        ref = fields[k]
        down = pltpu.make_async_remote_copy(
            ref.at[:, :, pl.ds(h, 8)], ref.at[:, :, pl.ds(0, 8)],
            halo_send.at[k, 0], halo_recv.at[k, 0], device_id=(ix + 1, iy), device_id_type=MESH)
        up = pltpu.make_async_remote_copy(
            ref.at[:, :, pl.ds(8, 8)], ref.at[:, :, pl.ds(h + 8, 8)],
            halo_send.at[k, 1], halo_recv.at[k, 1], device_id=(ix - 1, iy), device_id_type=MESH)
        east = pltpu.make_async_remote_copy(
            edge_out.at[k], edge_in.at[k, 0],
            col_send.at[k, 0], col_recv.at[k, 0], device_id=(ix, iy + 1), device_id_type=MESH)
        west = pltpu.make_async_remote_copy(
            edge_out.at[k], edge_in.at[k, 1],
            col_send.at[k, 1], col_recv.at[k, 1], device_id=(ix, iy - 1), device_id_type=MESH)
        return (has_s, down), (has_n, up), (has_e, east), (has_w, west)

    def start(there, copy):
        @pl.when(there)
        def _():
            copy.start()

    def send_rows(k):
        for there, copy in copies_of(k)[:2]:
            start(there, copy)

    def send_columns(k):
        ref = fields[k]
        lane = lax.broadcasted_iota(jnp.int32, (h, LT), 1)
        pack = pltpu.roll(ref[0, nt - 1, body], 1, 1)
        pack = jnp.where(lane == 7, pltpu.roll(ref[0, 0, body], 7, 1), pack)
        if ref.shape[0] == 2:
            pack = jnp.where(lane == 1, pltpu.roll(ref[1, nt - 1, body], 2, 1), pack)
            pack = jnp.where(lane == 6, pltpu.roll(ref[1, 0, body], 6, 1), pack)
        edge_out[k] = pack.T[:8]
        for there, copy in copies_of(k)[2:]:
            start(there, copy)

    def take_edges(k):
        (_, down), (_, up), (_, east), (_, west) = copies_of(k)
        for there, copy in ((has_w, east), (has_e, west), (has_n, down), (has_s, up)):

            @pl.when(there)
            def _(copy=copy):
                copy.wait_recv()

        row = lax.broadcasted_iota(jnp.int32, (8, h), 0)
        both = jnp.where(row < 4, edge_in[k, 0], edge_in[k, 1])
        halo[k] = jnp.concatenate([both] * (LT // 8), axis=0).T

    def drain_edges(k):
        for there, copy in copies_of(k):

            @pl.when(there)
            def _(copy=copy):
                copy.wait_send()

    def rows_of(step, first, last, stride=ROWS):
        def one(i, carry):
            step(pl.multiple_of(first + i * stride, ROWS))
            return carry

        lax.fori_loop(0, (last - first) // stride, one, 0, unroll=2)

    def border(step):
        rows_of(lambda r: step(r, outer), 0, h)
        rows_of(lambda r: step(r, inner), 0, 2 * (h - ROWS), h - ROWS)

    def interior(step):
        rows_of(lambda r: step(r, inner), ROWS, h - ROWS)

    lanes = lax.broadcasted_iota(jnp.int32, (ROWS, LT), 1)
    at_first, at_last = lanes == 0, lanes == LT - 1

    def cols(t):
        return pl.ds(t * LT, LT)

    def neighbours(k, c, r, t, kept):
        ref = fields[k]

        def turned(tile, by):
            if (c, tile, by) not in kept:
                kept[c, tile, by] = pltpu.roll(ref[c, tile, pl.ds(r + 8, ROWS)], by, 1)
            return kept[c, tile, by]

        def edge(by):
            value = halo[k, pl.ds(r, ROWS)]
            return pltpu.roll(value, by, 1) if c else value

        up = ref[c, t, pl.ds(r + 7, ROWS)]
        down = ref[c, t, pl.ds(r + 9, ROWS)]
        before = turned(t - 1, 1) if t else edge(LT - 1)
        after = turned(t + 1, LT - 1) if t < nt - 1 else edge(1)
        left = jnp.where(at_first, before, turned(t, 1))
        right = jnp.where(at_last, after, turned(t, LT - 1))
        return up, down, left, right

    def weighted(k, c, r, t, kept):
        up, down, left, right = neighbours(k, c, r, t, kept)
        ns, ew = up + down, left + right
        return 4.0 * ns + ew if c == 0 else ns + 4.0 * ew

    def viscosity(r, tiles):
        kept = {}
        for t in tiles:
            up, down, left, right = neighbours(0, 0, r, t, kept)
            ux, uy = down - up, right - left
            up, down, left, right = neighbours(0, 1, r, t, kept)
            vx, vy = down - up, right - left
            shear = uy + vx
            strain = 0.25 * (ux * ux + vy * vy + ux * vy + 0.25 * (shear * shear))
            here = pl.ds(r, ROWS)
            half = 0.5 * thick[here, cols(t)] * rate[here, cols(t)]
            root = half * lax.rsqrt(half) * jnp.exp2(jnp.log2(strain + 0.01) * (-1.0 / 6.0))
            s_pad[0, t, pl.ds(r + 8, ROWS)] = jnp.where(mask[here, cols(t)] >= 1, root, 0.0)

    def sources(r, tiles):
        here, there = pl.ds(r, ROWS), pl.ds(r + 8, ROWS)
        for t in tiles:
            kind = mask[here, cols(t)]
            s = s_pad[0, t, there]
            drag = jnp.where(kind == 2, fric[here, cols(t)], 0.0)
            fric[here, cols(t)] = drag
            code = codes[here, cols(t)] & 15
            pairs = code - (lax.shift_right_logical(code, 1) & 5)
            fronts = ((pairs & 3) + lax.shift_right_logical(pairs, 2)).astype(F32)
            e_f[here, cols(t)] = 2.0 * (s * s) * fronts + drag + 1.0
            for c in range(2):
                obs[c, here, cols(t)] = jnp.where(kind >= 1, vel[c, t, there] - obs[c, here, cols(t)], 0.0)

    def first(r, tiles):
        here, there = pl.ds(r, ROWS), pl.ds(r + 8, ROWS)
        kept = {}
        for t in tiles:
            up, down, left, right = neighbours(1, 0, r, t, kept)
            ns, ew = up + down, left + right
            s = s_pad[0, t, there]
            e = e_f[here, cols(t)]
            for c, total in ((0, 4.0 * ns + ew), (1, ns + 4.0 * ew)):
                inverse = 1.0 / (s * total + e)
                value = obs[c, here, cols(t)] * inverse
                p_f[c, here, cols(t)] = value
                g_f[c, here, cols(t)] = s * inverse
                q1[c, t, there] = s * value

    def second(r, tiles):
        here, there = pl.ds(r, ROWS), pl.ds(r + 8, ROWS)
        kept = {}
        for t in tiles:
            s = s_pad[0, t, there]
            for c in range(2):
                total = weighted(2, c, r, t, kept)
                q2[c, t, there] = q1[c, t, there] + s * g_f[c, here, cols(t)] * total

    def third(r, tiles):
        here, there = pl.ds(r, ROWS), pl.ds(r + 8, ROWS)
        kept = {}
        for t in tiles:
            flux = None
            for c in range(2):
                value = p_f[c, here, cols(t)] + g_f[c, here, cols(t)] * weighted(3, c, r, t, kept)
                adj[c, here, cols(t)] = value
                term = vel[c, t, there] * value
                flux = term if flux is None else flux + term
            grad[here, cols(t)] = (-fric[here, cols(t)] * flux).astype(BF16)

    for load in vel_loads:
        load.wait()
    send_rows(0)
    send_columns(0)
    for load in loads[:3]:
        load.wait()
    take_edges(0)
    border(viscosity)
    send_columns(1)
    send_rows(1)
    interior(viscosity)
    for load in loads[3:]:
        load.wait()
    rows_of(lambda r: sources(r, range(nt)), 0, h)
    mxt[...] = mx[...].T
    myt[...] = my[...].T.reshape(myt.shape)
    take_edges(1)
    border(first)
    send_columns(2)
    send_rows(2)
    interior(first)
    take_edges(2)
    border(second)
    send_columns(3)
    send_rows(3)
    interior(second)
    interior(third)
    take_edges(3)
    border(third)

    npc, nblk, kb, _ = r_acc.shape
    ab = npc * LT // ngx
    core = lax.rem(iy, 2)
    cell = iy // 2
    nbits = nblk.bit_length() - 1
    bits = [lax.rem(cell // (1 << t), 2) for t in range(nbits)]
    rows_dims = (((1,), (1,)), ((), ()))
    sent = []

    def project(side, p):
        rows = myt[:, side].reshape(nblk * kb, w)
        out = lax.dot_general(rows, t_hi[p], rows_dims, preferred_element_type=F32)
        out = out + lax.dot_general(rows, t_lo[p], rows_dims, preferred_element_type=F32)
        return out.reshape(nblk, kb, LT)

    pairs = []
    for p in range(npc):
        table = jnp.dot(mxt[p * LT : (p + 1) * LT, :], grad[...], preferred_element_type=F32)
        high = table.astype(BF16)
        t_hi[p] = high
        t_lo[p] = (table - high.astype(F32)).astype(BF16)
        r_send[p] = project(1 - core, p)
        pair = pltpu.make_async_remote_copy(
            r_send.at[p], r_in.at[p], pair_send.at[p], pair_recv.at[p],
            device_id=(ix, iy + 1 - 2 * core), device_id_type=MESH)
        pair.start()
        pairs.append(pair)

    live = [[] for _ in range(npc)]
    flying = [[] for _ in range(npc)]
    slot = 0
    for stage in range(nbits + 1):
        for p in range(npc):
            if stage == 0:
                r_acc[p] = project(core, p)
                pairs[p].wait_recv()
                r_acc[p] += r_in[p]
                sent.append(pairs[p])
            for copy, dst, place in flying[p]:
                copy.wait_recv()
                r_acc[p, dst] += half_in[place]
                sent.append(copy)
            flying[p] = []
            if stage < nbits:
                t = nbits - 1 - stage if p % 2 else stage
                free = [b for b in range(nbits) if b not in live[p] and b != t]
                for combo in range(1 << len(free)):
                    fixed = sum(((combo >> n) & 1) << b for n, b in enumerate(free))
                    fixed = fixed + sum((bits[b] * (1 << b) for b in live[p]), 0)
                    src = fixed + (1 - bits[t]) * (1 << t)
                    dst = fixed + bits[t] * (1 << t)
                    copy = pltpu.make_async_remote_copy(
                        r_acc.at[p, src], half_in.at[slot],
                        half_send.at[slot], half_recv.at[slot],
                        device_id=(ix, iy + (1 - 2 * bits[t]) * (2 << t)), device_id_type=MESH)
                    copy.start()
                    flying[p].append((copy, dst, slot))
                    slot += 1
                live[p].append(t)
            else:
                for d in range(p * LT // ab, (p + 1) * LT // ab):
                    z_out[d] = r_acc[p, cell, :, d * ab - p * LT : (d + 1) * ab - p * LT]

                    @pl.when(ix != d)
                    def _(d=d):
                        pltpu.make_async_remote_copy(
                            z_out.at[d], z_in.at[ix], z_send.at[d], z_recv.at[ix],
                            device_id=(d, iy), device_id_type=MESH).start()

    def z_copy(d):
        return pltpu.make_async_remote_copy(
            z_out.at[d], z_in.at[d], z_send.at[d], z_recv.at[d],
            device_id=(d, iy), device_id_type=MESH)

    coef_ref[...] = z_out[ix]
    for d in range(ngx):

        @pl.when(ix != d)
        def _(d=d):
            z_copy(d).wait_recv()
            coef_ref[...] += z_in[d]

    for d in range(ngx):

        @pl.when(ix != d)
        def _(d=d):
            z_copy(d).wait_send()

    for copy in sent:
        copy.wait_send()
    for k in range(4):
        drain_edges(k)


def write_results(adj, coef, adj_h, coef_h, adj_sem, coef_sem):
    rows = adj.shape[1] // 2
    copies = [pltpu.make_async_copy(coef, coef_h, coef_sem)]
    for n in range(4):
        part = (n % 2, pl.ds(n // 2 * rows, rows))
        copies.append(pltpu.make_async_copy(adj.at[part], adj_h.at[part], adj_sem.at[n]))
    for copy in copies:
        copy.start()
    for copy in copies:
        copy.wait()


def shards(ngx, ngy, velocity, observed, thickness, rate_factor, friction, cell_mask, front_codes, modes_x, modes_y):
    h, w = thickness.shape
    km = modes_x.shape[1]
    nblk, kb, ab = ngy // 2, km // ngy, km // ngx
    npc = km // LT
    slots = npc * sum(nblk >> (t + 1) for t in range(nblk.bit_length() - 1))
    hbm_spec = pl.BlockSpec(memory_space=pltpu.HBM)
    vmem_spec = pl.BlockSpec(memory_space=pltpu.VMEM)
    pad = (w // LT, h + 16, LT)
    dma = pltpu.SemaphoreType.DMA
    args = (velocity, observed, thickness, rate_factor, friction, cell_mask, front_codes, modes_x, modes_y)
    args = [pltpu.with_memory_space_constraint(x, pltpu.HBM) for x in args]
    adjoint, coefficients = pl.pallas_call(
        functools.partial(kernel, ngx, ngy),
        out_shape=(pltpu.VMEM((2, h, w), F32), pltpu.VMEM((kb, ab), F32)),
        in_specs=[hbm_spec] * 9,
        out_specs=(vmem_spec, vmem_spec),
        scratch_shapes=[
            pltpu.VMEM((2, *pad), F32),
            pltpu.VMEM((2, h, w), F32),
            pltpu.VMEM((h, w), F32),
            pltpu.VMEM((h, w), F32),
            pltpu.VMEM((h, w), F32),
            pltpu.VMEM((h, w), jnp.int32),
            pltpu.VMEM((h, w), jnp.int32),
            pltpu.VMEM((h, km), BF16),
            pltpu.VMEM((w, km), BF16),
            pltpu.VMEM((1, *pad), F32),
            pltpu.VMEM((2, *pad), F32),
            pltpu.VMEM((2, *pad), F32),
            pltpu.VMEM((2, h, w), F32),
            pltpu.VMEM((2, h, w), F32),
            pltpu.VMEM((h, w), F32),
            pltpu.VMEM((h, w), BF16),
            pltpu.VMEM((km, h), BF16),
            pltpu.VMEM((nblk, 2, kb, w), BF16),
            pltpu.VMEM((npc, LT, w), BF16),
            pltpu.VMEM((npc, LT, w), BF16),
            pltpu.VMEM((4, 8, h), F32),
            pltpu.VMEM((4, 2, 8, h), F32),
            pltpu.VMEM((4, h, LT), F32),
            pltpu.VMEM((npc, nblk, kb, LT), F32),
            pltpu.VMEM((npc, nblk, kb, LT), F32),
            pltpu.VMEM((npc, nblk, kb, LT), F32),
            pltpu.VMEM((slots, kb, LT), F32),
            pltpu.VMEM((ngx, kb, ab), F32),
            pltpu.VMEM((ngx, kb, ab), F32),
            dma((w // LT,)),
            dma((8,)),
            dma((4, 2)),
            dma((4, 2)),
            dma((4, 2)),
            dma((4, 2)),
            dma((npc,)),
            dma((npc,)),
            dma((slots,)),
            dma((slots,)),
            dma((ngx,)),
            dma((ngx,)),
        ],
        compiler_params=pltpu.CompilerParams(
            collective_id=0, has_side_effects=True, vmem_limit_bytes=VMEM_LIMIT
        ),
    )(*args)
    adjoint = pltpu.with_memory_space_constraint(adjoint, pltpu.VMEM)
    coefficients = pltpu.with_memory_space_constraint(coefficients, pltpu.VMEM)
    adjoint, coefficients = pl.pallas_call(
        write_results,
        out_shape=(
            jax.ShapeDtypeStruct((2, h, w), F32),
            jax.ShapeDtypeStruct((kb, ab), F32),
        ),
        in_specs=[vmem_spec, vmem_spec],
        out_specs=(hbm_spec, hbm_spec),
        scratch_shapes=[dma((4,)), dma],
    )(adjoint, coefficients)
    return adjoint, coefficients.T


def solution(mesh):
    tile = P("gx", "gy")
    pair = P(None, "gx", "gy")
    return jax.shard_map(
        functools.partial(shards, mesh.shape["gx"], mesh.shape["gy"]),
        mesh=mesh,
        in_specs=(pair, pair, tile, tile, tile, tile, tile, P("gx", None), P("gy", None)),
        out_specs=(pair, tile),
        check_vma=False,
    )
```

profile of v0, /device:TPU:0, one launch (start us, length us, event | category | flops | bytes accessed | tf_op | source)
XLA Modules:
  0.0 40.7 jit_solution(16133094571167837987)
XLA Ops:
  0.6 38.7 %shard_map.104 = (f32[2,512,512]{2,1,0:T(8,128)S(1)}, f32[64,128]{1,0:T(8,128)S(1)}) custom-call(f32[2,512,512]{2,1,0:T(8,128)} %vel_h.1, f32[2,512,512]{2,1,0:T(8,128)} %obs_h.1, f32[512,512]{1,0:T(8,128)} %thick_h.1, f32[512,512]{1,0:T(8,128)} %rate_h.1, f32[512,512]{1,0:T(8,128)} %fric_h.1, s32[512,512]{1,0:T(8,128)} %mask_h.1, s32[512,512]{1,0:T(8,128)} %codes_h.1, ...), custom_call_target="tpu_custom_call" | custom-call | tf_op jit(solution)/shard_map/pallas_call | solution.py:390
  39.3 1.4 %shard_map.105 = (f32[2,512,512]{2,1,0:T(8,128)}, f32[64,128]{1,0:T(8,128)}) custom-call(f32[2,512,512]{2,1,0:T(8,128)S(1)} %get-tuple-element.6.adj, f32[64,128]{1,0:T(8,128)S(1)} %get-tuple-element.7.coef), custom_call_target="tpu_custom_call" | custom-call | tf_op jit(solution)/shard_map/pallas_call | solution.py:444
where the time goes:
time: 40.8 us; the launch traced here: 40.7 us
  Pallas kernels  40.1 us (98%)
  between operations  0.64 us (2%)
    pallas_call x1, Pallas kernels, shards(): pl.pallas_call(functools.partial(kernel, ngx, ngy), out_shape=(pltpu.VMEM...  38.7 us
    pallas_call x1, Pallas kernels, shards(): pl.pallas_call(write_results, out_shape=(jax.ShapeDtypeStruct((2, h, w),...  1.37 us

commit v1 on v0

v1 whole, which is shorter than its diff:
```python
import functools

import jax
import jax.numpy as jnp
from jax import lax
from jax.experimental import pallas as pl
from jax.experimental.pallas import tpu as pltpu
from jax.sharding import PartitionSpec as P

SWEEPS = 3
LT = 128
LANES = 8
GROUPS = LT // LANES
TOP = 16
ROWS = 16
BLOCK = 128
FIELDS = 7
VMEM_LIMIT = 56 * 1024 * 1024
MESH = pl.DeviceIdType.MESH
F32 = jnp.float32
BF16 = jnp.bfloat16
U, V, ROOT, DRAG, FRONTS, RHS = 0, 1, 2, 3, 4, 5


def kernel(
    ngx, ngy,
    vel_h, obs_h, thick_h, rate_h, fric_h, mask_h, codes_h, mx_h, my_h,
    adj, coef_ref,
    d, raw_f, raw_i, mx, my, myt,
    ns_vel, ns_f, ns_i, pk_out, pk_in, corner_in,
    s_pad, q1, q2, p_f, g_f, grad,
    y_send, y_in, y_acc, g_in, z_out, z_in,
    load_sem, modes_sem, ns_send, ns_recv, pk_send, pk_recv, corner_send, corner_recv,
    y_ssem, y_rsem, g_ssem, g_rsem, z_send, z_recv,
):
    nt, h, _ = raw_i.shape[1:]
    w = nt * LT
    ring = nt + 1
    group = h // GROUPS
    ix, iy = lax.axis_index("gx"), lax.axis_index("gy")
    edge_tiles, inner_tiles = (0, nt - 1), tuple(range(1, nt - 1))

    def cols(t):
        return pl.ds(t * LT, LT)

    loads = {}
    for t in edge_tiles + inner_tiles:
        pairs = [
            (vel_h.at[:, :, cols(t)], d.at[pl.ds(U, 2), t, pl.ds(TOP, h)]),
            (obs_h.at[:, :, cols(t)], raw_f.at[pl.ds(3, 2), t]),
            (thick_h.at[:, cols(t)], raw_f.at[0, t]),
            (rate_h.at[:, cols(t)], raw_f.at[1, t]),
            (fric_h.at[:, cols(t)], raw_f.at[2, t]),
            (mask_h.at[:, cols(t)], raw_i.at[0, t]),
            (codes_h.at[:, cols(t)], raw_i.at[1, t]),
        ]
        loads[t] = [pltpu.make_async_copy(src, dst, load_sem.at[t, n]) for n, (src, dst) in enumerate(pairs)]
        for load in loads[t]:
            load.start()
    modes = [pltpu.make_async_copy(my_h, my, modes_sem.at[0]), pltpu.make_async_copy(mx_h, mx, modes_sem.at[1])]
    for load in modes:
        load.start()

    has_n, has_s, has_w, has_e = ix > 0, ix < ngx - 1, iy > 0, iy < ngy - 1
    diagonals = (
        (jnp.logical_and(has_n, has_w), -1, -1),
        (jnp.logical_and(has_n, has_e), -1, 1),
        (jnp.logical_and(has_s, has_w), 1, -1),
        (jnp.logical_and(has_s, has_e), 1, 1),
    )

    barrier = pltpu.get_barrier_semaphore()
    for off in range(1, ngx):
        pl.semaphore_signal(barrier, inc=1, device_id=(lax.rem(ix + off, ngx), iy), device_id_type=MESH)
    for off in range(1, ngy):
        pl.semaphore_signal(barrier, inc=1, device_id=(ix, lax.rem(iy + off, ngy)), device_id_type=MESH)
    near = 0
    for there, dx, dy in diagonals:
        near = near + there.astype(jnp.int32)

        @pl.when(there)
        def _(dx=dx, dy=dy):
            pl.semaphore_signal(barrier, inc=1, device_id=(ix + dx, iy + dy), device_id_type=MESH)

    pl.semaphore_wait(barrier, ngx - 1 + ngy - 1 + near)

    def row_copies(side):
        there, step = ((has_s, 1), (has_n, -1))[side]
        rows = pl.ds((h - 8, 0)[side], 8)
        pairs = [
            (vel_h.at[:, rows], ns_vel.at[side, pl.ds(0, 2)]),
            (obs_h.at[:, rows], ns_vel.at[side, pl.ds(2, 2)]),
            (thick_h.at[rows], ns_f.at[side, 0]),
            (rate_h.at[rows], ns_f.at[side, 1]),
            (fric_h.at[rows], ns_f.at[side, 2]),
            (mask_h.at[rows], ns_i.at[side, 0]),
            (codes_h.at[rows], ns_i.at[side, 1]),
        ]
        return there, [
            pltpu.make_async_remote_copy(
                src, dst, ns_send.at[side, n], ns_recv.at[side, n], device_id=(ix + step, iy), device_id_type=MESH)
            for n, (src, dst) in enumerate(pairs)
        ]

    def pack_copies():
        west = pltpu.make_async_remote_copy(
            pk_out.at[0], pk_in.at[1], pk_send.at[0], pk_recv.at[1], device_id=(ix, iy - 1), device_id_type=MESH)
        east = pltpu.make_async_remote_copy(
            pk_out.at[1], pk_in.at[0], pk_send.at[1], pk_recv.at[0], device_id=(ix, iy + 1), device_id_type=MESH)
        return [(has_w, west), (has_e, east)]

    def corner_copies():
        out = []
        for n, (there, dx, dy) in enumerate(diagonals):
            rows = pl.ds(0 if dx < 0 else group - 8, 8)
            out.append((there, pltpu.make_async_remote_copy(
                pk_out.at[0 if dy < 0 else 1, :, rows], corner_in.at[3 - n],
                corner_send.at[n], corner_recv.at[3 - n], device_id=(ix + dx, iy + dy), device_id_type=MESH)))
        return out

    for side in range(2):
        there, copies = row_copies(side)

        @pl.when(there)
        def _(copies=copies):
            for copy in copies:
                copy.start()

    for missing, side in ((ix == 0, 0), (ix == ngx - 1, 1)):

        @pl.when(missing)
        def _(side=side):
            ns_vel[side] = jnp.zeros(ns_vel.shape[1:], F32)
            ns_f[side] = jnp.zeros(ns_f.shape[1:], F32)
            ns_i[side] = jnp.zeros(ns_i.shape[1:], jnp.int32)

    for missing, side in ((iy == 0, 0), (iy == ngy - 1, 1)):

        @pl.when(missing)
        def _(side=side):
            pk_in[side] = jnp.zeros(pk_in.shape[1:], F32)

    for n, (there, _, _) in enumerate(diagonals):

        @pl.when(jnp.logical_not(there))
        def _(n=n):
            corner_in[n] = jnp.zeros(corner_in.shape[1:], F32)

    def loop(step, first, last, stride=ROWS, unroll=2):
        def one(i, carry):
            step(pl.multiple_of(first + i * stride, 8))
            return carry

        lax.fori_loop(0, (last - first) // stride, one, 0, unroll=unroll)

    def derive(kind, code, thick, rate, fric, vel, obs):
        half = 0.5 * thick * rate
        ice = kind >= 1
        root = jnp.where(ice, half * lax.rsqrt(half), 0.0)
        drag = jnp.where(kind == 2, fric, 0.0)
        pairs = code - (lax.shift_right_logical(code, 1) & 5)
        bits = (pairs & 3) + lax.shift_right_logical(pairs, 2)
        fronts = (2 * bits).astype(F32)
        return root, drag, fronts, jnp.where(ice, vel[0] - obs[0], 0.0), jnp.where(ice, vel[1] - obs[1], 0.0)

    def prepare(tiles):
        def step(r):
            here, there = pl.ds(r, ROWS), pl.ds(r + TOP, ROWS)
            for t in tiles:
                out = derive(
                    raw_i[0, t, here], raw_i[1, t, here], raw_f[0, t, here], raw_f[1, t, here], raw_f[2, t, here],
                    [d[U, t, there], d[V, t, there]], [raw_f[3, t, here], raw_f[4, t, here]])
                for f, value in enumerate(out):
                    d[ROOT + f, t, there] = value

        loop(step, 0, h)

    lane = lax.broadcasted_iota(jnp.int32, (group, LT), 1)
    lane8 = lax.broadcasted_iota(jnp.int32, (8, LT), 1)

    def pack(f, carry):
        for side, t in enumerate(edge_tiles):
            slot = lax.rem(lane + 4 * side, LT) // LANES
            value = None
            for n in range(GROUPS):
                part = d[f, t, pl.ds(TOP + n * group, group)]
                by = LANES * (n + 1) % LT
                part = pltpu.roll(part, by, 1) if by else part
                value = part if value is None else jnp.where(slot == (n + 1) % GROUPS, part, value)
            pk_out[side, f] = value
        return carry

    def unpack(f, carry):
        value = jnp.where(lane % LANES < 4, pk_in[1, f], pk_in[0, f])
        for n in range(GROUPS):
            by = (LT - LANES * (n + 1)) % LT
            d[f, nt, pl.ds(TOP + n * group, group)] = pltpu.roll(value, by, 1) if by else value
        d[f, nt, pl.ds(TOP - 8, 8)] = jnp.where(lane8 < LT // 2, corner_in[1, f], corner_in[0, f])
        low = jnp.where(lane8 % LANES < 4, corner_in[3, f], corner_in[2, f])
        d[f, nt, pl.ds(TOP + h, 8)] = pltpu.roll(low, LT - LANES, 1)
        return carry

    for t in edge_tiles:
        for load in loads[t]:
            load.wait()
    prepare(edge_tiles)
    lax.fori_loop(0, FIELDS, pack, 0)
    for there, copy in pack_copies() + corner_copies():

        @pl.when(there)
        def _(copy=copy):
            copy.start()

    for t in inner_tiles:
        for load in loads[t]:
            load.wait()
    prepare(inner_tiles)
    for load in modes:
        load.wait()
    myt[...] = my[...].T.reshape(myt.shape)

    for side, there in ((0, has_n), (1, has_s)):
        copies = row_copies(side)[1]

        @pl.when(there)
        def _(copies=copies):
            for copy in copies:
                copy.wait_recv()

        rows = pl.ds((TOP - 8, TOP + h)[side], 8)
        for t in range(nt):
            vel = [ns_vel[side, n, :, cols(t)] for n in range(2)]
            out = derive(
                ns_i[side, 0, :, cols(t)], ns_i[side, 1, :, cols(t)],
                ns_f[side, 0, :, cols(t)], ns_f[side, 1, :, cols(t)], ns_f[side, 2, :, cols(t)],
                vel, [ns_vel[side, 2 + n, :, cols(t)] for n in range(2)])
            for f, value in enumerate((*vel, *out)):
                d[f, t, rows] = value

    (_, west), (_, east) = pack_copies()
    for there, copy in ((has_w, east), (has_e, west)):

        @pl.when(there)
        def _(copy=copy):
            copy.wait_recv()

    for (there, _, _), (_, copy) in zip(diagonals, reversed(corner_copies())):

        @pl.when(there)
        def _(copy=copy):
            copy.wait_recv()

    lax.fori_loop(0, FIELDS, unpack, 0)

    lanes = lax.broadcasted_iota(jnp.int32, (ROWS, LT), 1)
    at_first, at_last = lanes == 0, lanes == LT - 1

    def neighbours(ref, c, r, t, kept):
        def turned(tile, by):
            tile = tile % ring
            if (c, tile, by) not in kept:
                kept[c, tile, by] = pltpu.roll(ref[c, tile, pl.ds(r, ROWS)], by, 1)
            return kept[c, tile, by]

        up = ref[c, t, pl.ds(r - 1, ROWS)]
        down = ref[c, t, pl.ds(r + 1, ROWS)]
        left = jnp.where(at_first, turned(t - 1, 1), turned(t, 1))
        right = jnp.where(at_last, turned(t + 1, LT - 1), turned(t, LT - 1))
        return up, down, left, right

    def weighted(ref, c, r, t, kept):
        up, down, left, right = neighbours(ref, c, r, t, kept)
        ns, ew = up + down, left + right
        return 4.0 * ns + ew if c == 0 else ns + 4.0 * ew

    def viscosity(r):
        kept = {}
        for t in range(ring):
            up, down, left, right = neighbours(d, U, r, t, kept)
            ux, uy = down - up, right - left
            up, down, left, right = neighbours(d, V, r, t, kept)
            vx, vy = down - up, right - left
            shear = uy + vx
            strain = 0.25 * (ux * ux + vy * vy + ux * vy + 0.25 * (shear * shear))
            s_pad[0, t, pl.ds(r, ROWS)] = d[ROOT, t, pl.ds(r, ROWS)] * jnp.exp2(jnp.log2(strain + 0.01) * (-1.0 / 6.0))

    def first(r):
        kept = {}
        here = pl.ds(r, ROWS)
        for t in range(ring):
            up, down, left, right = neighbours(s_pad, 0, r, t, kept)
            ns, ew = up + down, left + right
            s = s_pad[0, t, here]
            e = d[FRONTS, t, here] * (s * s) + d[DRAG, t, here] + 1.0
            for c, total in ((0, 4.0 * ns + ew), (1, ns + 4.0 * ew)):
                inverse = 1.0 / (s * total + e)
                value = d[RHS + c, t, here] * inverse
                p_f[c, t, here] = value
                g_f[c, t, here] = s * inverse
                q1[c, t, here] = s * value

    def second(r):
        kept = {}
        here = pl.ds(r, ROWS)
        for t in range(ring):
            s = s_pad[0, t, here]
            for c in range(2):
                q2[c, t, here] = q1[c, t, here] + s * g_f[c, t, here] * weighted(q1, c, r, t, kept)

    def third(r):
        kept = {}
        here, there = pl.ds(r - TOP, ROWS), pl.ds(r, ROWS)
        for t in range(nt):
            flux = None
            for c in range(2):
                value = p_f[c, t, there] + g_f[c, t, there] * weighted(q2, c, r, t, kept)
                adj[c, here, cols(t)] = value
                term = d[c, t, there] * value
                flux = term if flux is None else flux + term
            grad[here, cols(t)] = (-d[DRAG, t, there] * flux).astype(BF16)

    loop(viscosity, TOP - 8, TOP + h + 8, unroll=3)
    loop(first, TOP - 8, TOP + h + 8, unroll=3)
    loop(second, TOP - 8, TOP + h + 8, unroll=3)

    nblk, _, kb, _ = myt.shape
    steps = h // BLOCK
    ab = mx.shape[1] // ngx
    core = lax.rem(iy, 2)
    cell = iy // 2
    rows_dims = (((1,), (1,)), ((), ()))
    order = (nblk - 1, *range(1, nblk - 1))

    def project(side, k):
        rows = myt[:, side].reshape(nblk * kb, w)
        out = lax.dot_general(rows, grad[k * BLOCK : (k + 1) * BLOCK, :], rows_dims, preferred_element_type=F32)
        return out.reshape(nblk, kb, BLOCK)

    def sibling_copy(k):
        return pltpu.make_async_remote_copy(
            y_send.at[k], y_in.at[k], y_ssem.at[k], y_rsem.at[k],
            device_id=(ix, iy + 1 - 2 * core), device_id_type=MESH)

    def plane_copy(k, off):
        other = lax.rem(cell + off, nblk)
        return pltpu.make_async_remote_copy(
            y_acc.at[k, other], g_in.at[k, off - 1], g_ssem.at[k, off - 1], g_rsem.at[k, off - 1],
            device_id=(ix, 2 * other + core), device_id_type=MESH)

    def forward(k):
        sibling_copy(k).wait_recv()
        y_acc[k] += y_in[k]
        for off in range(nblk - 1, 0, -1):
            plane_copy(k, off).start()

    for k in range(steps):
        loop(third, TOP + k * BLOCK, TOP + (k + 1) * BLOCK, unroll=4)
        y_send[k] = project(1 - core, k)
        sibling_copy(k).start()
        y_acc[k] = project(core, k)
        if k:
            forward(k - 1)
    forward(steps - 1)

    total = None
    for k in range(steps):
        rows = y_acc[k, cell]
        for off in range(1, nblk):
            plane_copy(k, off).wait_recv()
            rows = rows + g_in[k, off - 1]
        high = rows.astype(BF16)
        low = (rows - high.astype(F32)).astype(BF16)
        both = jnp.concatenate([high, low], axis=0)
        out = jnp.dot(both, mx[k * BLOCK : (k + 1) * BLOCK, :], preferred_element_type=F32)
        total = out if total is None else total + out
    total = total[:kb] + total[kb:]

    for n in range(ngx):
        z_out[n] = total[:, n * ab : (n + 1) * ab]

    for n in range(ngx):

        @pl.when(ix != n)
        def _(n=n):
            pltpu.make_async_remote_copy(
                z_out.at[n], z_in.at[ix], z_send.at[n], z_recv.at[ix],
                device_id=(n, iy), device_id_type=MESH).start()

    def z_copy(n):
        return pltpu.make_async_remote_copy(
            z_out.at[n], z_in.at[n], z_send.at[n], z_recv.at[n],
            device_id=(n, iy), device_id_type=MESH)

    for side in range(2):
        there, copies = row_copies(side)

        @pl.when(there)
        def _(copies=copies):
            for copy in copies:
                copy.wait_send()

    for there, copy in pack_copies() + corner_copies():

        @pl.when(there)
        def _(copy=copy):
            copy.wait_send()

    for k in range(steps):
        sibling_copy(k).wait_send()
        for off in range(1, nblk):
            plane_copy(k, off).wait_send()

    coef_ref[...] = z_out[ix]
    for n in range(ngx):

        @pl.when(ix != n)
        def _(n=n):
            z_copy(n).wait_recv()
            coef_ref[...] += z_in[n]

    for n in range(ngx):

        @pl.when(ix != n)
        def _(n=n):
            z_copy(n).wait_send()


def write_results(adj, coef, adj_h, coef_h, adj_sem, coef_sem):
    rows = adj.shape[1] // 2
    copies = [pltpu.make_async_copy(coef, coef_h, coef_sem)]
    for n in range(4):
        part = (n % 2, pl.ds(n // 2 * rows, rows))
        copies.append(pltpu.make_async_copy(adj.at[part], adj_h.at[part], adj_sem.at[n]))
    for copy in copies:
        copy.start()
    for copy in copies:
        copy.wait()


def shards(ngx, ngy, velocity, observed, thickness, rate_factor, friction, cell_mask, front_codes, modes_x, modes_y):
    h, w = thickness.shape
    km = modes_x.shape[1]
    nt, nblk, kb, ab = w // LT, ngy // 2, km // ngy, km // ngx
    steps = h // BLOCK
    group = h // GROUPS
    hbm_spec = pl.BlockSpec(memory_space=pltpu.HBM)
    vmem_spec = pl.BlockSpec(memory_space=pltpu.VMEM)
    pad = (nt + 1, h + 2 * TOP, LT)
    dma = pltpu.SemaphoreType.DMA
    args = (velocity, observed, thickness, rate_factor, friction, cell_mask, front_codes, modes_x, modes_y)
    args = [pltpu.with_memory_space_constraint(x, pltpu.HBM) for x in args]
    adjoint, coefficients = pl.pallas_call(
        functools.partial(kernel, ngx, ngy),
        out_shape=(pltpu.VMEM((2, h, w), F32), pltpu.VMEM((kb, ab), F32)),
        in_specs=[hbm_spec] * 9,
        out_specs=(vmem_spec, vmem_spec),
        scratch_shapes=[
            pltpu.VMEM((FIELDS, *pad), F32),
            pltpu.VMEM((5, nt, h, LT), F32),
            pltpu.VMEM((2, nt, h, LT), jnp.int32),
            pltpu.VMEM((h, km), BF16),
            pltpu.VMEM((w, km), BF16),
            pltpu.VMEM((nblk, 2, kb, w), BF16),
            pltpu.VMEM((2, 4, 8, w), F32),
            pltpu.VMEM((2, 3, 8, w), F32),
            pltpu.VMEM((2, 2, 8, w), jnp.int32),
            pltpu.VMEM((2, FIELDS, group, LT), F32),
            pltpu.VMEM((2, FIELDS, group, LT), F32),
            pltpu.VMEM((4, FIELDS, 8, LT), F32),
            pltpu.VMEM((1, *pad), F32),
            pltpu.VMEM((2, *pad), F32),
            pltpu.VMEM((2, *pad), F32),
            pltpu.VMEM((2, *pad), F32),
            pltpu.VMEM((2, *pad), F32),
            pltpu.VMEM((h, w), BF16),
            pltpu.VMEM((steps, nblk, kb, BLOCK), F32),
            pltpu.VMEM((steps, nblk, kb, BLOCK), F32),
            pltpu.VMEM((steps, nblk, kb, BLOCK), F32),
            pltpu.VMEM((steps, nblk - 1, kb, BLOCK), F32),
            pltpu.VMEM((ngx, kb, ab), F32),
            pltpu.VMEM((ngx, kb, ab), F32),
            dma((nt, 7)),
            dma((2,)),
            dma((2, 7)),
            dma((2, 7)),
            dma((2,)),
            dma((2,)),
            dma((4,)),
            dma((4,)),
            dma((steps,)),
            dma((steps,)),
            dma((steps, nblk - 1)),
            dma((steps, nblk - 1)),
            dma((ngx,)),
            dma((ngx,)),
        ],
        compiler_params=pltpu.CompilerParams(
            collective_id=0, has_side_effects=True, vmem_limit_bytes=VMEM_LIMIT
        ),
    )(*args)
    adjoint = pltpu.with_memory_space_constraint(adjoint, pltpu.VMEM)
    coefficients = pltpu.with_memory_space_constraint(coefficients, pltpu.VMEM)
    adjoint, coefficients = pl.pallas_call(
        write_results,
        out_shape=(
            jax.ShapeDtypeStruct((2, h, w), F32),
            jax.ShapeDtypeStruct((kb, ab), F32),
        ),
        in_specs=[vmem_spec, vmem_spec],
        out_specs=(hbm_spec, hbm_spec),
        scratch_shapes=[dma((4,)), dma],
    )(adjoint, coefficients)
    return adjoint, coefficients.T


def solution(mesh):
    tile = P("gx", "gy")
    pair = P(None, "gx", "gy")
    return jax.shard_map(
        functools.partial(shards, mesh.shape["gx"], mesh.shape["gy"]),
        mesh=mesh,
        in_specs=(pair, pair, tile, tile, tile, tile, tile, P("gx", None), P("gy", None)),
        out_specs=(pair, tile),
        check_vma=False,
    )
```

time: 40.8 us -> 37.9 us (0.929)
  Pallas kernels: 40.1 us -> 37.1 us
    pallas_call x1, Pallas kernels: 38.7 us -> 35.8 us  [shards(): pl.pallas_call(functools.partial(kernel, ngx, ngy), out_shape=(pltpu.VMEM...]
where the time goes in v1:
time: 37.9 us; the launch traced here: 37.8 us
  Pallas kernels  37.1 us (98%)
  between operations  0.64 us (2%)
    pallas_call x1, Pallas kernels, shards(): pl.pallas_call(functools.partial(kernel, ngx, ngy), out_shape=(pltpu.VMEM...  35.8 us
    pallas_call x1, Pallas kernels, shards(): pl.pallas_call(write_results, out_shape=(jax.ShapeDtypeStruct((2, h, w),...  1.37 us

profile of v1, /device:TPU:0, one launch (start us, length us, event | category | flops | bytes accessed | tf_op | source)
XLA Modules:
  0.0 37.8 jit_solution(11679354232625473050)
XLA Ops:
  0.6 35.8 %shard_map.104 = (f32[2,512,512]{2,1,0:T(8,128)S(1)}, f32[64,128]{1,0:T(8,128)S(1)}) custom-call(f32[2,512,512]{2,1,0:T(8,128)} %vel_h.1, f32[2,512,512]{2,1,0:T(8,128)} %obs_h.1, f32[512,512]{1,0:T(8,128)} %thick_h.1, f32[512,512]{1,0:T(8,128)} %rate_h.1, f32[512,512]{1,0:T(8,128)} %fric_h.1, s32[512,512]{1,0:T(8,128)} %mask_h.1, s32[512,512]{1,0:T(8,128)} %codes_h.1, ...), custom_call_target="tpu_custom_call" | custom-call | tf_op jit(solution)/shard_map/pallas_call | solution.py:452
  36.4 1.4 %shard_map.105 = (f32[2,512,512]{2,1,0:T(8,128)}, f32[64,128]{1,0:T(8,128)}) custom-call(f32[2,512,512]{2,1,0:T(8,128)S(1)} %get-tuple-element.6.adj, f32[64,128]{1,0:T(8,128)S(1)} %get-tuple-element.7.coef), custom_call_target="tpu_custom_call" | custom-call | tf_op jit(solution)/shard_map/pallas_call | solution.py:503

commit v2 on v1

--- a/solution.py
+++ b/solution.py
@@ -55,6 +55,12 @@
             (codes_h.at[:, cols(t)], raw_i.at[1, t]),
         ]
         loads[t] = [pltpu.make_async_copy(src, dst, load_sem.at[t, n]) for n, (src, dst) in enumerate(pairs)]
+    for t in edge_tiles:
+        loads[t][0].start()
+    for t in edge_tiles:
+        for load in loads[t][1:]:
+            load.start()
+    for t in inner_tiles:
         for load in loads[t]:
             load.start()
     modes = [pltpu.make_async_copy(my_h, my, modes_sem.at[0]), pltpu.make_async_copy(mx_h, mx, modes_sem.at[1])]
@@ -81,8 +87,6 @@
         @pl.when(there)
         def _(dx=dx, dy=dy):
             pl.semaphore_signal(barrier, inc=1, device_id=(ix + dx, iy + dy), device_id_type=MESH)
-
-    pl.semaphore_wait(barrier, ngx - 1 + ngy - 1 + near)
 
     def row_copies(side):
         there, step = ((has_s, 1), (has_n, -1))[side]
@@ -102,29 +106,26 @@
             for n, (src, dst) in enumerate(pairs)
         ]
 
-    def pack_copies():
+    parts = (pl.ds(0, 2), pl.ds(2, FIELDS - 2))
+
+    def pack_copies(part):
         west = pltpu.make_async_remote_copy(
-            pk_out.at[0], pk_in.at[1], pk_send.at[0], pk_recv.at[1], device_id=(ix, iy - 1), device_id_type=MESH)
+            pk_out.at[0, parts[part]], pk_in.at[1, parts[part]], pk_send.at[part, 0], pk_recv.at[part, 1],
+            device_id=(ix, iy - 1), device_id_type=MESH)
         east = pltpu.make_async_remote_copy(
-            pk_out.at[1], pk_in.at[0], pk_send.at[1], pk_recv.at[0], device_id=(ix, iy + 1), device_id_type=MESH)
+            pk_out.at[1, parts[part]], pk_in.at[0, parts[part]], pk_send.at[part, 1], pk_recv.at[part, 0],
+            device_id=(ix, iy + 1), device_id_type=MESH)
         return [(has_w, west), (has_e, east)]
 
-    def corner_copies():
+    def corner_copies(part):
         out = []
         for n, (there, dx, dy) in enumerate(diagonals):
             rows = pl.ds(0 if dx < 0 else group - 8, 8)
             out.append((there, pltpu.make_async_remote_copy(
-                pk_out.at[0 if dy < 0 else 1, :, rows], corner_in.at[3 - n],
-                corner_send.at[n], corner_recv.at[3 - n], device_id=(ix + dx, iy + dy), device_id_type=MESH)))
+                pk_out.at[0 if dy < 0 else 1, parts[part], rows], corner_in.at[3 - n, parts[part]],
+                corner_send.at[part, n], corner_recv.at[part, 3 - n],
+                device_id=(ix + dx, iy + dy), device_id_type=MESH)))
         return out
-
-    for side in range(2):
-        there, copies = row_copies(side)
-
-        @pl.when(there)
-        def _(copies=copies):
-            for copy in copies:
-                copy.start()
 
     for missing, side in ((ix == 0, 0), (ix == ngx - 1, 1)):
 
@@ -145,6 +146,9 @@
         @pl.when(jnp.logical_not(there))
         def _(n=n):
             corner_in[n] = jnp.zeros(corner_in.shape[1:], F32)
+
+    def aligned(r, by):
+        return r if isinstance(r, int) else pl.multiple_of(r, by)
 
     def loop(step, first, last, stride=ROWS, unroll=2):
         def one(i, carry):
@@ -173,7 +177,7 @@
                 for f, value in enumerate(out):
                     d[ROOT + f, t, there] = value
 
-        loop(step, 0, h)
+        loop(step, 0, h, unroll=4)
 
     lane = lax.broadcasted_iota(jnp.int32, (group, LT), 1)
     lane8 = lax.broadcasted_iota(jnp.int32, (8, LT), 1)
@@ -200,58 +204,6 @@
         d[f, nt, pl.ds(TOP + h, 8)] = pltpu.roll(low, LT - LANES, 1)
         return carry
 
-    for t in edge_tiles:
-        for load in loads[t]:
-            load.wait()
-    prepare(edge_tiles)
-    lax.fori_loop(0, FIELDS, pack, 0)
-    for there, copy in pack_copies() + corner_copies():
-
-        @pl.when(there)
-        def _(copy=copy):
-            copy.start()
-
-    for t in inner_tiles:
-        for load in loads[t]:
-            load.wait()
-    prepare(inner_tiles)
-    for load in modes:
-        load.wait()
-    myt[...] = my[...].T.reshape(myt.shape)
-
-    for side, there in ((0, has_n), (1, has_s)):
-        copies = row_copies(side)[1]
-
-        @pl.when(there)
-        def _(copies=copies):
-            for copy in copies:
-                copy.wait_recv()
-
-        rows = pl.ds((TOP - 8, TOP + h)[side], 8)
-        for t in range(nt):
-            vel = [ns_vel[side, n, :, cols(t)] for n in range(2)]
-            out = derive(
-                ns_i[side, 0, :, cols(t)], ns_i[side, 1, :, cols(t)],
-                ns_f[side, 0, :, cols(t)], ns_f[side, 1, :, cols(t)], ns_f[side, 2, :, cols(t)],
-                vel, [ns_vel[side, 2 + n, :, cols(t)] for n in range(2)])
-            for f, value in enumerate((*vel, *out)):
-                d[f, t, rows] = value
-
-    (_, west), (_, east) = pack_copies()
-    for there, copy in ((has_w, east), (has_e, west)):
-
-        @pl.when(there)
-        def _(copy=copy):
-            copy.wait_recv()
-
-    for (there, _, _), (_, copy) in zip(diagonals, reversed(corner_copies())):
-
-        @pl.when(there)
-        def _(copy=copy):
-            copy.wait_recv()
-
-    lax.fori_loop(0, FIELDS, unpack, 0)
-
     lanes = lax.broadcasted_iota(jnp.int32, (ROWS, LT), 1)
     at_first, at_last = lanes == 0, lanes == LT - 1
 
@@ -282,7 +234,8 @@
             vx, vy = down - up, right - left
             shear = uy + vx
             strain = 0.25 * (ux * ux + vy * vy + ux * vy + 0.25 * (shear * shear))
-            s_pad[0, t, pl.ds(r, ROWS)] = d[ROOT, t, pl.ds(r, ROWS)] * jnp.exp2(jnp.log2(strain + 0.01) * (-1.0 / 6.0))
+            factor = jnp.exp2(jnp.log2(strain + 0.01) * (-1.0 / 6.0))
+            s_pad[0, t, pl.ds(r, ROWS)] = d[ROOT, t, pl.ds(r, ROWS)] * factor if t < nt else factor
 
     def first(r):
         kept = {}
@@ -309,7 +262,7 @@
 
     def third(r):
         kept = {}
-        here, there = pl.ds(r - TOP, ROWS), pl.ds(r, ROWS)
+        here, there = pl.ds(aligned(r - TOP, ROWS), ROWS), pl.ds(r, ROWS)
         for t in range(nt):
             flux = None
             for c in range(2):
@@ -319,10 +272,6 @@
                 flux = term if flux is None else flux + term
             grad[here, cols(t)] = (-d[DRAG, t, there] * flux).astype(BF16)
 
-    loop(viscosity, TOP - 8, TOP + h + 8, unroll=3)
-    loop(first, TOP - 8, TOP + h + 8, unroll=3)
-    loop(second, TOP - 8, TOP + h + 8, unroll=3)
-
     nblk, _, kb, _ = myt.shape
     steps = h // BLOCK
     ab = mx.shape[1] // ngx
@@ -333,7 +282,8 @@
 
     def project(side, k):
         rows = myt[:, side].reshape(nblk * kb, w)
-        out = lax.dot_general(rows, grad[k * BLOCK : (k + 1) * BLOCK, :], rows_dims, preferred_element_type=F32)
+        here = pl.ds(pl.multiple_of(k * BLOCK, BLOCK), BLOCK)
+        out = lax.dot_general(rows, grad[here, :], rows_dims, preferred_element_type=F32)
         return out.reshape(nblk, kb, BLOCK)
 
     def sibling_copy(k):
@@ -353,14 +303,138 @@
         for off in range(nblk - 1, 0, -1):
             plane_copy(k, off).start()
 
-    for k in range(steps):
-        loop(third, TOP + k * BLOCK, TOP + (k + 1) * BLOCK, unroll=4)
+    def start_sides(part):
+        for there, copy in pack_copies(part) + corner_copies(part):
+
+            @pl.when(there)
+            def _(copy=copy):
+                copy.start()
+
+    def take_sides(part):
+        (_, west), (_, east) = pack_copies(part)
+        waits = [(has_w, east), (has_e, west)]
+        waits += [(there, copy) for (there, _, _), (_, copy) in zip(diagonals, reversed(corner_copies(part)))]
+        for there, copy in waits:
+
+            @pl.when(there)
+            def _(copy=copy):
+                copy.wait_recv()
+
+    for t in edge_tiles:
+        loads[t][0].wait()
+    lax.fori_loop(0, 2, pack, 0)
+    pl.semaphore_wait(barrier, ngx - 1 + ngy - 1 + near)
+    start_sides(0)
+    for side in range(2):
+        there, copies = row_copies(side)
+
+        @pl.when(there)
+        def _(copies=copies):
+            for copy in copies:
+                copy.start()
+
+    for t in edge_tiles:
+        for load in loads[t][1:]:
+            load.wait()
+    prepare(edge_tiles)
+    lax.fori_loop(2, FIELDS, pack, 0)
+    start_sides(1)
+
+    for t in inner_tiles:
+        for load in loads[t]:
+            load.wait()
+    prepare(inner_tiles)
+    for load in modes:
+        load.wait()
+    myt[...] = my[...].T.reshape(myt.shape)
+
+    take_sides(0)
+    lax.fori_loop(0, 2, unpack, 0)
+    loop(viscosity, TOP + 8, TOP + h - 8, unroll=8)
+
+    for side, there in ((0, has_n), (1, has_s)):
+        copies = row_copies(side)[1]
+
+        @pl.when(there)
+        def _(copies=copies):
+            for copy in copies:
+                copy.wait_recv()
+
+        rows = pl.ds((TOP - 8, TOP + h)[side], 8)
+        for t in range(nt):
+            vel = [ns_vel[side, n, :, cols(t)] for n in range(2)]
+            out = derive(
+                ns_i[side, 0, :, cols(t)], ns_i[side, 1, :, cols(t)],
+                ns_f[side, 0, :, cols(t)], ns_f[side, 1, :, cols(t)], ns_f[side, 2, :, cols(t)],
+                vel, [ns_vel[side, 2 + n, :, cols(t)] for n in range(2)])
+            for f, value in enumerate((*vel, *out)):
+                d[f, t, rows] = value
+
+    viscosity(TOP - 8)
+    viscosity(TOP + h - 8)
+
+    take_sides(1)
+    lax.fori_loop(2, FIELDS, unpack, 0)
+    ringed = pl.ds(TOP - 8, h + 16)
+    s_pad[0, nt, ringed] = s_pad[0, nt, ringed] * d[ROOT, nt, ringed]
+
+    def wave(n, parts="tsf"):
+        if "t" in parts:
+            third(aligned(TOP + (n - 4) * ROWS, ROWS))
+        if "s" in parts:
+            second(aligned(TOP - 8 + (n - 2) * ROWS, 8))
+        if "f" in parts:
+            first(aligned(TOP - 8 + n * ROWS, 8))
+
+    per = BLOCK // ROWS
+    half = per // 2
+
+    def send_half(k):
         y_send[k] = project(1 - core, k)
-        sibling_copy(k).start()
+
+    def keep_half(k):
         y_acc[k] = project(core, k)
-        if k:
-            forward(k - 1)
-    forward(steps - 1)
+
+    for n in range(4):
+        wave(n, "f" if n < 2 else "sf")
+
+    def opening(i, carry):
+        for n in range(half):
+            wave(4 + i * half + n)
+        return carry
+
+    lax.fori_loop(0, 2, opening, 0)
+
+    def block(k, carry):
+        send_half(k - 1)
+        for n in range(half):
+            wave(4 + k * per + n)
+        sibling_copy(k - 1).start()
+
+        @pl.when(k >= 2)
+        def _():
+            forward(k - 2)
+
+        keep_half(k - 1)
+        for n in range(half):
+            wave(4 + k * per + half + n)
+        return carry
+
+    lax.fori_loop(1, steps - 1, block, 0)
+    last = steps - 1
+    send_half(last - 1)
+    for n in range(half):
+        wave(4 + last * per + n)
+    sibling_copy(last - 1).start()
+    forward(last - 2)
+    keep_half(last - 1)
+    for n, parts_of in enumerate(("tsf", "ts", "ts", "t")):
+        wave(4 + last * per + half + n, parts_of)
+    send_half(last)
+    sibling_copy(last).start()
+    forward(last - 1)
+    keep_half(last)
+    forward(last)
 
     total = None
     for k in range(steps):
@@ -399,7 +473,7 @@
             for copy in copies:
                 copy.wait_send()
 
-    for there, copy in pack_copies() + corner_copies():
+    for there, copy in pack_copies(0) + corner_copies(0) + pack_copies(1) + corner_copies(1):
 
         @pl.when(there)
         def _(copy=copy):
@@ -483,10 +557,10 @@
             dma((2,)),
             dma((2, 7)),
             dma((2, 7)),
-            dma((2,)),
-            dma((2,)),
-            dma((4,)),
-            dma((4,)),
+            dma((2, 2)),
+            dma((2, 2)),
+            dma((2, 4)),
+            dma((2, 4)),
             dma((steps,)),
             dma((steps,)),
             dma((steps, nblk - 1)),

time: 37.9 us -> 31.9 us (0.84)
  Pallas kernels: 37.1 us -> 31.1 us
    pallas_call x1, Pallas kernels: 35.8 us -> 29.8 us  [shards(): pl.pallas_call(functools.partial(kernel, ngx, ngy), out_shape=(pltpu.VMEM...]
where the time goes in v2:
time: 31.9 us; the launch traced here: 31.8 us
  Pallas kernels  31.1 us (97%)
  between operations  0.64 us (2%)
    pallas_call x1, Pallas kernels, shards(): pl.pallas_call(functools.partial(kernel, ngx, ngy), out_shape=(pltpu.VMEM...  29.8 us
    pallas_call x1, Pallas kernels, shards(): pl.pallas_call(write_results, out_shape=(jax.ShapeDtypeStruct((2, h, w),...  1.37 us

profile of v2, /device:TPU:0, one launch (start us, length us, event | category | flops | bytes accessed | tf_op | source)
XLA Modules:
  0.0 31.8 jit_solution(18207189837177976511)
XLA Ops:
  0.6 29.8 %shard_map.104 = (f32[2,512,512]{2,1,0:T(8,128)S(1)}, f32[64,128]{1,0:T(8,128)S(1)}) custom-call(f32[2,512,512]{2,1,0:T(8,128)} %vel_h.1, f32[2,512,512]{2,1,0:T(8,128)} %obs_h.1, f32[512,512]{1,0:T(8,128)} %thick_h.1, f32[512,512]{1,0:T(8,128)} %rate_h.1, f32[512,512]{1,0:T(8,128)} %fric_h.1, s32[512,512]{1,0:T(8,128)} %mask_h.1, s32[512,512]{1,0:T(8,128)} %codes_h.1, ...), custom_call_target="tpu_custom_call" | custom-call | tf_op jit(solution)/shard_map/pallas_call | solution.py:526
  30.4 1.4 %shard_map.105 = (f32[2,512,512]{2,1,0:T(8,128)}, f32[64,128]{1,0:T(8,128)}) custom-call(f32[2,512,512]{2,1,0:T(8,128)S(1)} %get-tuple-element.6.adj, f32[64,128]{1,0:T(8,128)S(1)} %get-tuple-element.7.coef), custom_call_target="tpu_custom_call" | custom-call | tf_op jit(solution)/shard_map/pallas_call | solution.py:577

commit v3 on v2

--- a/solution.py
+++ b/solution.py
@@ -9,11 +9,13 @@
 
 SWEEPS = 3
 LT = 128
-LANES = 8
+DEEP = 4
+LANES = 2 * DEEP
 GROUPS = LT // LANES
 TOP = 16
 ROWS = 16
 BLOCK = 128
+EARLY = 2
 FIELDS = 7
 VMEM_LIMIT = 56 * 1024 * 1024
 MESH = pl.DeviceIdType.MESH
@@ -55,14 +57,15 @@
             (codes_h.at[:, cols(t)], raw_i.at[1, t]),
         ]
         loads[t] = [pltpu.make_async_copy(src, dst, load_sem.at[t, n]) for n, (src, dst) in enumerate(pairs)]
+    rigid, extra = (2, 3, 5), (1, 4, 6)
     for t in edge_tiles:
         loads[t][0].start()
-    for t in edge_tiles:
-        for load in loads[t][1:]:
-            load.start()
-    for t in inner_tiles:
-        for load in loads[t]:
-            load.start()
+    for n in range(1, 7):
+        for t in edge_tiles:
+            loads[t][n].start()
+    for n in (0, *rigid, *extra):
+        for t in inner_tiles:
+            loads[t][n].start()
     modes = [pltpu.make_async_copy(my_h, my, modes_sem.at[0]), pltpu.make_async_copy(mx_h, mx, modes_sem.at[1])]
     for load in modes:
         load.start()
@@ -90,15 +93,15 @@
 
     def row_copies(side):
         there, step = ((has_s, 1), (has_n, -1))[side]
-        rows = pl.ds((h - 8, 0)[side], 8)
+        rows, to = pl.ds((h - DEEP, 0)[side], DEEP), pl.ds((8 - DEEP, 0)[side], DEEP)
         pairs = [
-            (vel_h.at[:, rows], ns_vel.at[side, pl.ds(0, 2)]),
-            (obs_h.at[:, rows], ns_vel.at[side, pl.ds(2, 2)]),
-            (thick_h.at[rows], ns_f.at[side, 0]),
-            (rate_h.at[rows], ns_f.at[side, 1]),
-            (fric_h.at[rows], ns_f.at[side, 2]),
-            (mask_h.at[rows], ns_i.at[side, 0]),
-            (codes_h.at[rows], ns_i.at[side, 1]),
+            (vel_h.at[:, rows], ns_vel.at[side, pl.ds(0, 2), to]),
+            (obs_h.at[:, rows], ns_vel.at[side, pl.ds(2, 2), to]),
+            (thick_h.at[rows], ns_f.at[side, 0, to]),
+            (rate_h.at[rows], ns_f.at[side, 1, to]),
+            (fric_h.at[rows], ns_f.at[side, 2, to]),
+            (mask_h.at[rows], ns_i.at[side, 0, to]),
+            (codes_h.at[rows], ns_i.at[side, 1, to]),
         ]
         return there, [
             pltpu.make_async_remote_copy(
@@ -110,10 +113,10 @@
 
     def pack_copies(part):
         west = pltpu.make_async_remote_copy(
-            pk_out.at[0, parts[part]], pk_in.at[1, parts[part]], pk_send.at[part, 0], pk_recv.at[part, 1],
+            pk_out.at[parts[part]], pk_in.at[1, parts[part]], pk_send.at[part, 0], pk_recv.at[part, 1],
             device_id=(ix, iy - 1), device_id_type=MESH)
         east = pltpu.make_async_remote_copy(
-            pk_out.at[1, parts[part]], pk_in.at[0, parts[part]], pk_send.at[part, 1], pk_recv.at[part, 0],
+            pk_out.at[parts[part]], pk_in.at[0, parts[part]], pk_send.at[part, 1], pk_recv.at[part, 0],
             device_id=(ix, iy + 1), device_id_type=MESH)
         return [(has_w, west), (has_e, east)]
 
@@ -122,7 +125,7 @@
         for n, (there, dx, dy) in enumerate(diagonals):
             rows = pl.ds(0 if dx < 0 else group - 8, 8)
             out.append((there, pltpu.make_async_remote_copy(
-                pk_out.at[0 if dy < 0 else 1, parts[part], rows], corner_in.at[3 - n, parts[part]],
+                pk_out.at[parts[part], rows], corner_in.at[3 - n, parts[part]],
                 corner_send.at[part, n], corner_recv.at[part, 3 - n],
                 device_id=(ix + dx, iy + dy), device_id_type=MESH)))
         return out
@@ -157,67 +160,76 @@
 
         lax.fori_loop(0, (last - first) // stride, one, 0, unroll=unroll)
 
-    def derive(kind, code, thick, rate, fric, vel, obs):
+    def root_of(kind, thick, rate):
         half = 0.5 * thick * rate
+        return jnp.where(kind >= 1, half * lax.rsqrt(half), 0.0)
+
+    def derive(kind, code, fric, vel, obs):
         ice = kind >= 1
-        root = jnp.where(ice, half * lax.rsqrt(half), 0.0)
         drag = jnp.where(kind == 2, fric, 0.0)
         pairs = code - (lax.shift_right_logical(code, 1) & 5)
         bits = (pairs & 3) + lax.shift_right_logical(pairs, 2)
         fronts = (2 * bits).astype(F32)
-        return root, drag, fronts, jnp.where(ice, vel[0] - obs[0], 0.0), jnp.where(ice, vel[1] - obs[1], 0.0)
-
-    def prepare(tiles):
+        return drag, fronts, jnp.where(ice, vel[0] - obs[0], 0.0), jnp.where(ice, vel[1] - obs[1], 0.0)
+
+    def raw_root(t, r, rows):
+        here = pl.ds(r, rows)
+        return root_of(raw_i[0, t, here], raw_f[0, t, here], raw_f[1, t, here])
+
+    def edge_root(side, t):
+        return root_of(ns_i[side, 0, :, cols(t)], ns_f[side, 0, :, cols(t)], ns_f[side, 1, :, cols(t)])
+
+    def prepare(tiles, rooted):
         def step(r):
             here, there = pl.ds(r, ROWS), pl.ds(r + TOP, ROWS)
             for t in tiles:
+                if rooted:
+                    d[ROOT, t, there] = raw_root(t, r, ROWS)
                 out = derive(
-                    raw_i[0, t, here], raw_i[1, t, here], raw_f[0, t, here], raw_f[1, t, here], raw_f[2, t, here],
+                    raw_i[0, t, here], raw_i[1, t, here], raw_f[2, t, here],
                     [d[U, t, there], d[V, t, there]], [raw_f[3, t, here], raw_f[4, t, here]])
                 for f, value in enumerate(out):
-                    d[ROOT + f, t, there] = value
-
-        loop(step, 0, h, unroll=4)
+                    d[DRAG + f, t, there] = value
+
+        loop(step, 0, h, unroll=8)
 
     lane = lax.broadcasted_iota(jnp.int32, (group, LT), 1)
     lane8 = lax.broadcasted_iota(jnp.int32, (8, LT), 1)
-
-    def pack(f, carry):
-        for side, t in enumerate(edge_tiles):
-            slot = lax.rem(lane + 4 * side, LT) // LANES
-            value = None
-            for n in range(GROUPS):
-                part = d[f, t, pl.ds(TOP + n * group, group)]
-                by = LANES * (n + 1) % LT
-                part = pltpu.roll(part, by, 1) if by else part
-                value = part if value is None else jnp.where(slot == (n + 1) % GROUPS, part, value)
-            pk_out[side, f] = value
-        return carry
-
-    def unpack(f, carry):
-        value = jnp.where(lane % LANES < 4, pk_in[1, f], pk_in[0, f])
+    slot = lax.rem(lane + LANES // 2, LT) // LANES
+
+    def pack(f):
+        value = None
+        for n in range(GROUPS):
+            here = pl.ds(TOP + n * group, group)
+            part = jnp.where(lane < LT // 2, d[f, 0, here], d[f, nt - 1, here])
+            by = LANES * (n + 1) % LT
+            part = pltpu.roll(part, by, 1) if by else part
+            value = part if value is None else jnp.where(slot == (n + 1) % GROUPS, part, value)
+        pk_out[f] = value
+
+    def unpack(f):
+        value = jnp.where(lane % LANES < DEEP, pk_in[1, f], pk_in[0, f])
         for n in range(GROUPS):
             by = (LT - LANES * (n + 1)) % LT
             d[f, nt, pl.ds(TOP + n * group, group)] = pltpu.roll(value, by, 1) if by else value
         d[f, nt, pl.ds(TOP - 8, 8)] = jnp.where(lane8 < LT // 2, corner_in[1, f], corner_in[0, f])
-        low = jnp.where(lane8 % LANES < 4, corner_in[3, f], corner_in[2, f])
+        low = jnp.where(lane8 % LANES < DEEP, corner_in[3, f], corner_in[2, f])
         d[f, nt, pl.ds(TOP + h, 8)] = pltpu.roll(low, LT - LANES, 1)
-        return carry
-
-    lanes = lax.broadcasted_iota(jnp.int32, (ROWS, LT), 1)
-    at_first, at_last = lanes == 0, lanes == LT - 1
-
-    def neighbours(ref, c, r, t, kept):
+
+
+    def neighbours(ref, c, r, t, kept, rows=ROWS):
+        lanes = lax.broadcasted_iota(jnp.int32, (rows, LT), 1)
+
         def turned(tile, by):
             tile = tile % ring
             if (c, tile, by) not in kept:
-                kept[c, tile, by] = pltpu.roll(ref[c, tile, pl.ds(r, ROWS)], by, 1)
+                kept[c, tile, by] = pltpu.roll(ref[c, tile, pl.ds(r, rows)], by, 1)
             return kept[c, tile, by]
 
-        up = ref[c, t, pl.ds(r - 1, ROWS)]
-        down = ref[c, t, pl.ds(r + 1, ROWS)]
-        left = jnp.where(at_first, turned(t - 1, 1), turned(t, 1))
-        right = jnp.where(at_last, turned(t + 1, LT - 1), turned(t, LT - 1))
+        up = ref[c, t, pl.ds(r - 1, rows)]
+        down = ref[c, t, pl.ds(r + 1, rows)]
+        left = jnp.where(lanes == 0, turned(t - 1, 1), turned(t, 1))
+        right = jnp.where(lanes == LT - 1, turned(t + 1, LT - 1), turned(t, LT - 1))
         return up, down, left, right
 
     def weighted(ref, c, r, t, kept):
@@ -225,17 +237,26 @@
         ns, ew = up + down, left + right
         return 4.0 * ns + ew if c == 0 else ns + 4.0 * ew
 
-    def viscosity(r):
+    def viscosity(r, rows=ROWS, side=None):
         kept = {}
+        here = pl.ds(r, rows)
         for t in range(ring):
-            up, down, left, right = neighbours(d, U, r, t, kept)
+            up, down, left, right = neighbours(d, U, r, t, kept, rows)
             ux, uy = down - up, right - left
-            up, down, left, right = neighbours(d, V, r, t, kept)
+            up, down, left, right = neighbours(d, V, r, t, kept, rows)
             vx, vy = down - up, right - left
             shear = uy + vx
             strain = 0.25 * (ux * ux + vy * vy + ux * vy + 0.25 * (shear * shear))
             factor = jnp.exp2(jnp.log2(strain + 0.01) * (-1.0 / 6.0))
-            s_pad[0, t, pl.ds(r, ROWS)] = d[ROOT, t, pl.ds(r, ROWS)] * factor if t < nt else factor
+            if t < nt:
+                if side is not None:
+                    root = edge_root(side, t)
+                elif t in edge_tiles:
+                    root = d[ROOT, t, here]
+                else:
+                    root = raw_root(t, aligned(r - TOP, 8), rows)
+                factor = root * factor
+            s_pad[0, t, here] = factor
 
     def first(r):
         kept = {}
@@ -322,7 +343,8 @@
 
     for t in edge_tiles:
         loads[t][0].wait()
-    lax.fori_loop(0, 2, pack, 0)
+    pack(U)
+    pack(V)
     pl.semaphore_wait(barrier, ngx - 1 + ngy - 1 + near)
     start_sides(0)
     for side in range(2):
@@ -336,21 +358,28 @@
     for t in edge_tiles:
         for load in loads[t][1:]:
             load.wait()
-    prepare(edge_tiles)
-    lax.fori_loop(2, FIELDS, pack, 0)
+    prepare(edge_tiles, True)
+    for f in range(2, FIELDS):
+        pack(f)
     start_sides(1)
 
-    for t in inner_tiles:
-        for load in loads[t]:
-            load.wait()
-    prepare(inner_tiles)
+    for n in (0, *rigid):
+        for t in inner_tiles:
+            loads[t][n].wait()
+    take_sides(0)
+    unpack(U)
+    unpack(V)
+    tall = (h // ROWS - 2) * ROWS
+    loop(viscosity, TOP + 8, TOP + 8 + tall, unroll=10)
+    viscosity(TOP + 8 + tall)
+
+    for n in extra:
+        for t in inner_tiles:
+            loads[t][n].wait()
+    prepare(inner_tiles, False)
     for load in modes:
         load.wait()
     myt[...] = my[...].T.reshape(myt.shape)
-
-    take_sides(0)
-    lax.fori_loop(0, 2, unpack, 0)
-    loop(viscosity, TOP + 8, TOP + h - 8, unroll=8)
 
     for side, there in ((0, has_n), (1, has_s)):
         copies = row_copies(side)[1]
@@ -364,17 +393,18 @@
         for t in range(nt):
             vel = [ns_vel[side, n, :, cols(t)] for n in range(2)]
             out = derive(
-                ns_i[side, 0, :, cols(t)], ns_i[side, 1, :, cols(t)],
-                ns_f[side, 0, :, cols(t)], ns_f[side, 1, :, cols(t)], ns_f[side, 2, :, cols(t)],
+                ns_i[side, 0, :, cols(t)], ns_i[side, 1, :, cols(t)], ns_f[side, 2, :, cols(t)],
                 vel, [ns_vel[side, 2 + n, :, cols(t)] for n in range(2)])
-            for f, value in enumerate((*vel, *out)):
+            for f, value in zip((U, V, DRAG, FRONTS, RHS, RHS + 1), (*vel, *out)):
                 d[f, t, rows] = value
 
-    viscosity(TOP - 8)
-    viscosity(TOP + h - 8)
+    for side, r in ((0, TOP), (1, TOP + h - 8)):
+        viscosity(r, 8)
+        viscosity((r - 8, r + 8)[side], 8, side)
 
     take_sides(1)
-    lax.fori_loop(2, FIELDS, unpack, 0)
+    for f in range(2, FIELDS):
+        unpack(f)
     ringed = pl.ds(TOP - 8, h + 16)
     s_pad[0, nt, ringed] = s_pad[0, nt, ringed] * d[ROOT, nt, ringed]
 
@@ -407,7 +437,7 @@
 
     def block(k, carry):
         send_half(k - 1)
-        for n in range(half):
+        for n in range(EARLY):
             wave(4 + k * per + n)
         sibling_copy(k - 1).start()
 
@@ -416,20 +446,20 @@
             forward(k - 2)
 
         keep_half(k - 1)
-        for n in range(half):
-            wave(4 + k * per + half + n)
+        for n in range(EARLY, per):
+            wave(4 + k * per + n)
         return carry
 
     lax.fori_loop(1, steps - 1, block, 0)
     last = steps - 1
     send_half(last - 1)
-    for n in range(half):
+    for n in range(EARLY):
         wave(4 + last * per + n)
     sibling_copy(last - 1).start()
     forward(last - 2)
     keep_half(last - 1)
-    for n, parts_of in enumerate(("tsf", "ts", "ts", "t")):
-        wave(4 + last * per + half + n, parts_of)
+    for n in range(EARLY, per):
+        wave(4 + last * per + n, {per - 3: "ts", per - 2: "ts", per - 1: "t"}.get(n, "tsf"))
     send_half(last)
     sibling_copy(last).start()
     forward(last - 1)
@@ -452,13 +482,14 @@
     for n in range(ngx):
         z_out[n] = total[:, n * ab : (n + 1) * ab]
 
-    for n in range(ngx):
-
-        @pl.when(ix != n)
-        def _(n=n):
-            pltpu.make_async_remote_copy(
-                z_out.at[n], z_in.at[ix], z_send.at[n], z_recv.at[ix],
-                device_id=(n, iy), device_id_type=MESH).start()
+    for off in range(ngx - 1, 0, -1):
+        for n in (ix - off, ix + off):
+
+            @pl.when(jnp.logical_and(n >= 0, n < ngx))
+            def _(n=n):
+                pltpu.make_async_remote_copy(
+                    z_out.at[n], z_in.at[ix], z_send.at[n], z_recv.at[ix],
+                    device_id=(n, iy), device_id_type=MESH).start()
 
     def z_copy(n):
         return pltpu.make_async_remote_copy(
@@ -538,7 +569,7 @@
             pltpu.VMEM((2, 4, 8, w), F32),
             pltpu.VMEM((2, 3, 8, w), F32),
             pltpu.VMEM((2, 2, 8, w), jnp.int32),
-            pltpu.VMEM((2, FIELDS, group, LT), F32),
+            pltpu.VMEM((FIELDS, group, LT), F32),
             pltpu.VMEM((2, FIELDS, group, LT), F32),
             pltpu.VMEM((4, FIELDS, 8, LT), F32),
             pltpu.VMEM((1, *pad), F32),

time: 31.9 us -> 30.7 us (0.962)
  Pallas kernels: 31.1 us -> 29.9 us
    pallas_call x1, Pallas kernels: 29.8 us -> 28.6 us  [shards(): pl.pallas_call(functools.partial(kernel, ngx, ngy), out_shape=(pltpu.VMEM...]
where the time goes in v3:
time: 30.7 us; the launch traced here: 30.6 us
  Pallas kernels  29.9 us (97%)
  between operations  0.64 us (2%)
    pallas_call x1, Pallas kernels, shards(): pl.pallas_call(functools.partial(kernel, ngx, ngy), out_shape=(pltpu.VMEM...  28.6 us
    pallas_call x1, Pallas kernels, shards(): pl.pallas_call(write_results, out_shape=(jax.ShapeDtypeStruct((2, h, w),...  1.37 us

profile of v3, /device:TPU:0, one launch (start us, length us, event | category | flops | bytes accessed | tf_op | source)
XLA Modules:
  0.0 30.6 jit_solution(15514507786343812707)
XLA Ops:
  0.6 28.6 %shard_map.104 = (f32[2,512,512]{2,1,0:T(8,128)S(1)}, f32[64,128]{1,0:T(8,128)S(1)}) custom-call(f32[2,512,512]{2,1,0:T(8,128)} %vel_h.1, f32[2,512,512]{2,1,0:T(8,128)} %obs_h.1, f32[512,512]{1,0:T(8,128)} %thick_h.1, f32[512,512]{1,0:T(8,128)} %rate_h.1, f32[512,512]{1,0:T(8,128)} %fric_h.1, s32[512,512]{1,0:T(8,128)} %mask_h.1, s32[512,512]{1,0:T(8,128)} %codes_h.1, ...), custom_call_target="tpu_custom_call" | custom-call | tf_op jit(solution)/shard_map/pallas_call | solution.py:557
  29.2 1.4 %shard_map.105 = (f32[2,512,512]{2,1,0:T(8,128)}, f32[64,128]{1,0:T(8,128)}) custom-call(f32[2,512,512]{2,1,0:T(8,128)S(1)} %get-tuple-element.6.adj, f32[64,128]{1,0:T(8,128)S(1)} %get-tuple-element.7.coef), custom_call_target="tpu_custom_call" | custom-call | tf_op jit(solution)/shard_map/pallas_call | solution.py:608

commit v4 on v3

--- a/solution.py
+++ b/solution.py
@@ -44,6 +44,27 @@
 
     def cols(t):
         return pl.ds(t * LT, LT)
+
+    has_n, has_s, has_w, has_e = ix > 0, ix < ngx - 1, iy > 0, iy < ngy - 1
+    diagonals = (
+        (jnp.logical_and(has_n, has_w), -1, -1),
+        (jnp.logical_and(has_n, has_e), -1, 1),
+        (jnp.logical_and(has_s, has_w), 1, -1),
+        (jnp.logical_and(has_s, has_e), 1, 1),
+    )
+
+    barrier = pltpu.get_barrier_semaphore()
+    for off in range(1, ngx):
+        pl.semaphore_signal(barrier, inc=1, device_id=(lax.rem(ix + off, ngx), iy), device_id_type=MESH)
+    for off in range(1, ngy):
+        pl.semaphore_signal(barrier, inc=1, device_id=(ix, lax.rem(iy + off, ngy)), device_id_type=MESH)
+    near = 0
+    for there, dx, dy in diagonals:
+        near = near + there.astype(jnp.int32)
+
+        @pl.when(there)
+        def _(dx=dx, dy=dy):
+            pl.semaphore_signal(barrier, inc=1, device_id=(ix + dx, iy + dy), device_id_type=MESH)
 
     loads = {}
     for t in edge_tiles + inner_tiles:
@@ -70,27 +91,6 @@
     for load in modes:
         load.start()
 
-    has_n, has_s, has_w, has_e = ix > 0, ix < ngx - 1, iy > 0, iy < ngy - 1
-    diagonals = (
-        (jnp.logical_and(has_n, has_w), -1, -1),
-        (jnp.logical_and(has_n, has_e), -1, 1),
-        (jnp.logical_and(has_s, has_w), 1, -1),
-        (jnp.logical_and(has_s, has_e), 1, 1),
-    )
-
-    barrier = pltpu.get_barrier_semaphore()
-    for off in range(1, ngx):
-        pl.semaphore_signal(barrier, inc=1, device_id=(lax.rem(ix + off, ngx), iy), device_id_type=MESH)
-    for off in range(1, ngy):
-        pl.semaphore_signal(barrier, inc=1, device_id=(ix, lax.rem(iy + off, ngy)), device_id_type=MESH)
-    near = 0
-    for there, dx, dy in diagonals:
-        near = near + there.astype(jnp.int32)
-
-        @pl.when(there)
-        def _(dx=dx, dy=dy):
-            pl.semaphore_signal(barrier, inc=1, device_id=(ix + dx, iy + dy), device_id_type=MESH)
-
     def row_copies(side):
         there, step = ((has_s, 1), (has_n, -1))[side]
         rows, to = pl.ds((h - DEEP, 0)[side], DEEP), pl.ds((8 - DEEP, 0)[side], DEEP)
@@ -217,33 +217,29 @@
         d[f, nt, pl.ds(TOP + h, 8)] = pltpu.roll(low, LT - LANES, 1)
 
 
-    def neighbours(ref, c, r, t, kept, rows=ROWS):
+    def neighbours(ref, c, r, t, rows=ROWS):
         lanes = lax.broadcasted_iota(jnp.int32, (rows, LT), 1)
 
-        def turned(tile, by):
-            tile = tile % ring
-            if (c, tile, by) not in kept:
-                kept[c, tile, by] = pltpu.roll(ref[c, tile, pl.ds(r, rows)], by, 1)
-            return kept[c, tile, by]
+        def near(tile):
+            return ref[c, tile % ring, pl.ds(r, rows)]
 
         up = ref[c, t, pl.ds(r - 1, rows)]
         down = ref[c, t, pl.ds(r + 1, rows)]
-        left = jnp.where(lanes == 0, turned(t - 1, 1), turned(t, 1))
-        right = jnp.where(lanes == LT - 1, turned(t + 1, LT - 1), turned(t, LT - 1))
+        left = pltpu.roll(jnp.where(lanes == LT - 1, near(t - 1), near(t)), 1, 1)
+        right = pltpu.roll(jnp.where(lanes == 0, near(t + 1), near(t)), LT - 1, 1)
         return up, down, left, right
 
-    def weighted(ref, c, r, t, kept):
-        up, down, left, right = neighbours(ref, c, r, t, kept)
+    def weighted(ref, c, r, t):
+        up, down, left, right = neighbours(ref, c, r, t)
         ns, ew = up + down, left + right
         return 4.0 * ns + ew if c == 0 else ns + 4.0 * ew
 
-    def viscosity(r, rows=ROWS, side=None):
-        kept = {}
+    def viscosity(r, rows=ROWS, side=None, tiles=tuple(range(ring))):
         here = pl.ds(r, rows)
-        for t in range(ring):
-            up, down, left, right = neighbours(d, U, r, t, kept, rows)
+        for t in tiles:
+            up, down, left, right = neighbours(d, U, r, t, rows)
             ux, uy = down - up, right - left
-            up, down, left, right = neighbours(d, V, r, t, kept, rows)
+            up, down, left, right = neighbours(d, V, r, t, rows)
             vx, vy = down - up, right - left
             shear = uy + vx
             strain = 0.25 * (ux * ux + vy * vy + ux * vy + 0.25 * (shear * shear))
@@ -259,10 +255,9 @@
             s_pad[0, t, here] = factor
 
     def first(r):
-        kept = {}
         here = pl.ds(r, ROWS)
         for t in range(ring):
-            up, down, left, right = neighbours(s_pad, 0, r, t, kept)
+            up, down, left, right = neighbours(s_pad, 0, r, t)
             ns, ew = up + down, left + right
             s = s_pad[0, t, here]
             e = d[FRONTS, t, here] * (s * s) + d[DRAG, t, here] + 1.0
@@ -274,20 +269,18 @@
                 q1[c, t, here] = s * value
 
     def second(r):
-        kept = {}
         here = pl.ds(r, ROWS)
         for t in range(ring):
             s = s_pad[0, t, here]
             for c in range(2):
-                q2[c, t, here] = q1[c, t, here] + s * g_f[c, t, here] * weighted(q1, c, r, t, kept)
+                q2[c, t, here] = q1[c, t, here] + s * g_f[c, t, here] * weighted(q1, c, r, t)
 
     def third(r):
-        kept = {}
         here, there = pl.ds(aligned(r - TOP, ROWS), ROWS), pl.ds(r, ROWS)
         for t in range(nt):
             flux = None
             for c in range(2):
-                value = p_f[c, t, there] + g_f[c, t, there] * weighted(q2, c, r, t, kept)
+                value = p_f[c, t, there] + g_f[c, t, there] * weighted(q2, c, r, t)
                 adj[c, here, cols(t)] = value
                 term = d[c, t, there] * value
                 flux = term if flux is None else flux + term
@@ -299,7 +292,6 @@
     core = lax.rem(iy, 2)
     cell = iy // 2
     rows_dims = (((1,), (1,)), ((), ()))
-    order = (nblk - 1, *range(1, nblk - 1))
 
     def project(side, k):
         rows = myt[:, side].reshape(nblk * kb, w)
@@ -313,7 +305,10 @@
             device_id=(ix, iy + 1 - 2 * core), device_id_type=MESH)
 
     def plane_copy(k, off):
-        other = lax.rem(cell + off, nblk)
+        other = cell
+        for bit in range(nblk.bit_length() - 1):
+            if off >> bit & 1:
+                other = other + (1 - 2 * lax.rem(cell // (1 << bit), 2)) * (1 << bit)
         return pltpu.make_async_remote_copy(
             y_acc.at[k, other], g_in.at[k, off - 1], g_ssem.at[k, off - 1], g_rsem.at[k, off - 1],
             device_id=(ix, 2 * other + core), device_id_type=MESH)
@@ -366,13 +361,14 @@
     for n in (0, *rigid):
         for t in inner_tiles:
             loads[t][n].wait()
-    take_sides(0)
-    unpack(U)
-    unpack(V)
     tall = (h // ROWS - 2) * ROWS
-    loop(viscosity, TOP + 8, TOP + 8 + tall, unroll=10)
-    viscosity(TOP + 8 + tall)
-
+    outer = (nt - 1, nt, 0)
+
+    def rough(tiles):
+        loop(lambda r: viscosity(r, tiles=tiles), TOP + 8, TOP + 8 + tall, unroll=10)
+        viscosity(TOP + 8 + tall, tiles=tiles)
+
+    rough(inner_tiles)
     for n in extra:
         for t in inner_tiles:
             loads[t][n].wait()
@@ -380,6 +376,11 @@
     for load in modes:
         load.wait()
     myt[...] = my[...].T.reshape(myt.shape)
+
+    take_sides(0)
+    unpack(U)
+    unpack(V)
+    rough(outer)
 
     for side, there in ((0, has_n), (1, has_s)):
         copies = row_copies(side)[1]
@@ -428,12 +429,8 @@
     for n in range(4):
         wave(n, "f" if n < 2 else "sf")
 
-    def opening(i, carry):
-        for n in range(half):
-            wave(4 + i * half + n)
-        return carry
-
-    lax.fori_loop(0, 2, opening, 0)
+    for n in range(per):
+        wave(4 + n)
 
     def block(k, carry):
         send_half(k - 1)

time: 30.7 us -> 29.9 us (0.974)
  Pallas kernels: 29.9 us -> 29.1 us
    pallas_call x1, Pallas kernels: 28.6 us -> 27.7 us  [shards(): pl.pallas_call(functools.partial(kernel, ngx, ngy), out_shape=(pltpu.VMEM...]
where the time goes in v4:
time: 29.9 us; the launch traced here: 29.7 us
  Pallas kernels  29.1 us (97%)
  between operations  0.64 us (2%)
    pallas_call x1, Pallas kernels, shards(): pl.pallas_call(functools.partial(kernel, ngx, ngy), out_shape=(pltpu.VMEM...  27.7 us
    pallas_call x1, Pallas kernels, shards(): pl.pallas_call(write_results, out_shape=(jax.ShapeDtypeStruct((2, h, w),...  1.37 us

profile of v4, /device:TPU:0, one launch (start us, length us, event | category | flops | bytes accessed | tf_op | source)
XLA Modules:
  0.0 29.7 jit_solution(5435539291221110353)
XLA Ops:
  0.6 27.7 %shard_map.104 = (f32[2,512,512]{2,1,0:T(8,128)S(1)}, f32[64,128]{1,0:T(8,128)S(1)}) custom-call(f32[2,512,512]{2,1,0:T(8,128)} %vel_h.1, f32[2,512,512]{2,1,0:T(8,128)} %obs_h.1, f32[512,512]{1,0:T(8,128)} %thick_h.1, f32[512,512]{1,0:T(8,128)} %rate_h.1, f32[512,512]{1,0:T(8,128)} %fric_h.1, s32[512,512]{1,0:T(8,128)} %mask_h.1, s32[512,512]{1,0:T(8,128)} %codes_h.1, ...), custom_call_target="tpu_custom_call" | custom-call | tf_op jit(solution)/shard_map/pallas_call | solution.py:554
  28.4 1.4 %shard_map.105 = (f32[2,512,512]{2,1,0:T(8,128)}, f32[64,128]{1,0:T(8,128)}) custom-call(f32[2,512,512]{2,1,0:T(8,128)S(1)} %get-tuple-element.6.adj, f32[64,128]{1,0:T(8,128)S(1)} %get-tuple-element.7.coef), custom_call_target="tpu_custom_call" | custom-call | tf_op jit(solution)/shard_map/pallas_call | solution.py:605

commit v5 on v4

--- a/solution.py
+++ b/solution.py
@@ -123,9 +123,10 @@
     def corner_copies(part):
         out = []
         for n, (there, dx, dy) in enumerate(diagonals):
-            rows = pl.ds(0 if dx < 0 else group - 8, 8)
+            rows = pl.ds(0 if dx < 0 else group - DEEP, DEEP)
+            to = pl.ds(0 if dx < 0 else 8 - DEEP, DEEP)
             out.append((there, pltpu.make_async_remote_copy(
-                pk_out.at[parts[part], rows], corner_in.at[3 - n, parts[part]],
+                pk_out.at[parts[part], rows], corner_in.at[3 - n, parts[part], to],
                 corner_send.at[part, n], corner_recv.at[part, 3 - n],
                 device_id=(ix + dx, iy + dy), device_id_type=MESH)))
         return out
@@ -304,19 +305,23 @@
             y_send.at[k], y_in.at[k], y_ssem.at[k], y_rsem.at[k],
             device_id=(ix, iy + 1 - 2 * core), device_id_type=MESH)
 
-    def plane_copy(k, off):
+    def partner(off):
         other = cell
         for bit in range(nblk.bit_length() - 1):
             if off >> bit & 1:
                 other = other + (1 - 2 * lax.rem(cell // (1 << bit), 2)) * (1 << bit)
+        return other
+
+    def plane_copy(k, off):
+        other = partner(off)
         return pltpu.make_async_remote_copy(
             y_acc.at[k, other], g_in.at[k, off - 1], g_ssem.at[k, off - 1], g_rsem.at[k, off - 1],
             device_id=(ix, 2 * other + core), device_id_type=MESH)
 
     def forward(k):
         sibling_copy(k).wait_recv()
-        y_acc[k] += y_in[k]
         for off in range(nblk - 1, 0, -1):
+            y_acc[k, partner(off)] += y_in[k, partner(off)]
             plane_copy(k, off).start()
 
     def start_sides(part):
@@ -432,22 +437,17 @@
     for n in range(per):
         wave(4 + n)
 
-    def block(k, carry):
+    for k in range(1, steps - 1):
         send_half(k - 1)
         for n in range(EARLY):
             wave(4 + k * per + n)
         sibling_copy(k - 1).start()
-
-        @pl.when(k >= 2)
-        def _():
+        if k >= 2:
             forward(k - 2)
-
         keep_half(k - 1)
         for n in range(EARLY, per):
             wave(4 + k * per + n)
-        return carry
-
-    lax.fori_loop(1, steps - 1, block, 0)
+
     last = steps - 1
     send_half(last - 1)
     for n in range(EARLY):
@@ -465,7 +465,7 @@
 
     total = None
     for k in range(steps):
-        rows = y_acc[k, cell]
+        rows = y_acc[k, cell] + y_in[k, cell]
         for off in range(1, nblk):
             plane_copy(k, off).wait_recv()
             rows = rows + g_in[k, off - 1]

time: 29.9 us -> 29 us (0.970)
  Pallas kernels: 29.1 us -> 28.2 us
    pallas_call x1, Pallas kernels: 27.7 us -> 26.9 us  [shards(): pl.pallas_call(functools.partial(kernel, ngx, ngy), out_shape=(pltpu.VMEM...]
where the time goes in v5:
time: 29 us; the launch traced here: 28.9 us
  Pallas kernels  28.2 us (97%)
  between operations  0.64 us (2%)
    pallas_call x1, Pallas kernels, shards(): pl.pallas_call(functools.partial(kernel, ngx, ngy), out_shape=(pltpu.VMEM...  26.9 us
    pallas_call x1, Pallas kernels, shards(): pl.pallas_call(write_results, out_shape=(jax.ShapeDtypeStruct((2, h, w),...  1.37 us

profile of v5, /device:TPU:0, one launch (start us, length us, event | category | flops | bytes accessed | tf_op | source)
XLA Modules:
  0.0 28.9 jit_solution(6817267795160058072)
XLA Ops:
  0.6 26.9 %shard_map.104 = (f32[2,512,512]{2,1,0:T(8,128)S(1)}, f32[64,128]{1,0:T(8,128)S(1)}) custom-call(f32[2,512,512]{2,1,0:T(8,128)} %vel_h.1, f32[2,512,512]{2,1,0:T(8,128)} %obs_h.1, f32[512,512]{1,0:T(8,128)} %thick_h.1, f32[512,512]{1,0:T(8,128)} %rate_h.1, f32[512,512]{1,0:T(8,128)} %fric_h.1, s32[512,512]{1,0:T(8,128)} %mask_h.1, s32[512,512]{1,0:T(8,128)} %codes_h.1, ...), custom_call_target="tpu_custom_call" | custom-call | tf_op jit(solution)/shard_map/pallas_call | solution.py:554
  27.5 1.4 %shard_map.105 = (f32[2,512,512]{2,1,0:T(8,128)}, f32[64,128]{1,0:T(8,128)}) custom-call(f32[2,512,512]{2,1,0:T(8,128)S(1)} %get-tuple-element.6.adj, f32[64,128]{1,0:T(8,128)S(1)} %get-tuple-element.7.coef), custom_call_target="tpu_custom_call" | custom-call | tf_op jit(solution)/shard_map/pallas_call | solution.py:605

commit v6 on v5

--- a/solution.py
+++ b/solution.py
@@ -94,14 +94,15 @@
     def row_copies(side):
         there, step = ((has_s, 1), (has_n, -1))[side]
         rows, to = pl.ds((h - DEEP, 0)[side], DEEP), pl.ds((8 - DEEP, 0)[side], DEEP)
+        few, few_to = pl.ds((h - 2, 0)[side], 2), pl.ds((6, 0)[side], 2)
         pairs = [
             (vel_h.at[:, rows], ns_vel.at[side, pl.ds(0, 2), to]),
-            (obs_h.at[:, rows], ns_vel.at[side, pl.ds(2, 2), to]),
+            (obs_h.at[:, few], ns_vel.at[side, pl.ds(2, 2), few_to]),
             (thick_h.at[rows], ns_f.at[side, 0, to]),
             (rate_h.at[rows], ns_f.at[side, 1, to]),
-            (fric_h.at[rows], ns_f.at[side, 2, to]),
+            (fric_h.at[few], ns_f.at[side, 2, few_to]),
             (mask_h.at[rows], ns_i.at[side, 0, to]),
-            (codes_h.at[rows], ns_i.at[side, 1, to]),
+            (codes_h.at[few], ns_i.at[side, 1, few_to]),
         ]
         return there, [
             pltpu.make_async_remote_copy(

time: 29 us -> 29.1 us (level)
  no operation moved by 1% of the time
where the time goes in v6:
time: 29.1 us; the launch traced here: 28.9 us
  Pallas kernels  28.3 us (97%)
  between operations  0.64 us (2%)
    pallas_call x1, Pallas kernels, shards(): pl.pallas_call(functools.partial(kernel, ngx, ngy), out_shape=(pltpu.VMEM...  26.9 us
    pallas_call x1, Pallas kernels, shards(): pl.pallas_call(write_results, out_shape=(jax.ShapeDtypeStruct((2, h, w),...  1.37 us

profile of v6, /device:TPU:0, one launch (start us, length us, event | category | flops | bytes accessed | tf_op | source)
XLA Modules:
  0.0 28.9 jit_solution(9184262869806475980)
XLA Ops:
  0.6 26.9 %shard_map.104 = (f32[2,512,512]{2,1,0:T(8,128)S(1)}, f32[64,128]{1,0:T(8,128)S(1)}) custom-call(f32[2,512,512]{2,1,0:T(8,128)} %vel_h.1, f32[2,512,512]{2,1,0:T(8,128)} %obs_h.1, f32[512,512]{1,0:T(8,128)} %thick_h.1, f32[512,512]{1,0:T(8,128)} %rate_h.1, f32[512,512]{1,0:T(8,128)} %fric_h.1, s32[512,512]{1,0:T(8,128)} %mask_h.1, s32[512,512]{1,0:T(8,128)} %codes_h.1, ...), custom_call_target="tpu_custom_call" | custom-call | tf_op jit(solution)/shard_map/pallas_call | solution.py:555
  27.5 1.4 %shard_map.105 = (f32[2,512,512]{2,1,0:T(8,128)}, f32[64,128]{1,0:T(8,128)}) custom-call(f32[2,512,512]{2,1,0:T(8,128)S(1)} %get-tuple-element.6.adj, f32[64,128]{1,0:T(8,128)S(1)} %get-tuple-element.7.coef), custom_call_target="tpu_custom_call" | custom-call | tf_op jit(solution)/shard_map/pallas_call | solution.py:606
